TPU v7x, 256 devices: a whole 4x4x8 slice. The times are simulated.
256 devices in a mesh: dp: 8 (over x, z_hi), dap: 32 (over z_lo, y, core).
Axes of the slice: x: 4, y: 4, z: 8 (z_hi: 2, z_lo: 4; z = z_hi * 4 + z_lo), core: 2. Of those that a mesh axis runs over, the one named last changes fastest.
Arguments:
- pair_rep: bfloat16 [2048, 256, 128], P(('dp', 'dap')), parts along dimension 0, may hold values from -6 to 6
- cotangent: bfloat16 [2048, 256, 128], P(('dp', 'dap')), parts along dimension 0, may hold values from -6 to 6
- norm_gain: float32 [2, 128], replicated, may hold values from 0.5 to 1.5
- w_project: float32 [2, 128, 512], replicated, may hold values from -3 to 3
- w_bias: float32 [2, 128, 4], replicated, may hold values from -0.5 to 0.5
- w_out: float32 [2, 128, 128], replicated, may hold values from -0.5 to 0.5
Outputs:
- d_pair: bfloat16 [2048, 256, 128], P(('dp', 'dap')), parts along dimension 0
- grad_gain: float32 [16, 128], P('dp'), parts along dimension 0
- grad_project: float32 [16, 128, 512], P('dp'), parts along dimension 0
- grad_bias: float32 [16, 128, 4], P('dp'), parts along dimension 0
- grad_out: float32 [16, 128, 128], P('dp'), parts along dimension 0
There are 8 independent parts, one for each index of `dp`. A program takes and returns all parts, laid end to end along the dimension named above; an argument that names none is the same for every part. Nothing has to cross between parts.
All inputs are finite; a program needn't handle non-finite values.
Results may differ from a plain program's by a relative error of at most 0.02.
The roundings to bfloat16 on the way count: a program that leaves them out, or rounds other values in their place, can miss the bound.
Values may be sent and summed in bfloat16 or wider, within the bound.
A program may use at most 64 MiB of HBM per device.

v0:
```python
import jax
import jax.numpy as jnp
from jax import lax
from jax.sharding import PartitionSpec as P

EPS = 1e-05


def as_sent(shard):

    def short(part):
        return part.astype(jnp.bfloat16) if part.dtype == jnp.float32 else part

    return jax.tree.map(short, shard)


def normalize(values_f, gain):
    row_mean = jnp.mean(values_f, axis=-1, keepdims=True)
    centred = values_f - row_mean
    variance = jnp.mean(centred * centred, axis=-1, keepdims=True)
    return centred * lax.rsqrt(variance + EPS) * gain


def project(pair_rows, gain, w_project, w_bias):
    normed = normalize(pair_rows.astype(jnp.float32), gain).astype(jnp.bfloat16)
    projected = jnp.einsum(
        "rnc,cf->rnf", normed, w_project.astype(jnp.bfloat16), preferred_element_type=jnp.float32
    )
    bias_rows = jnp.einsum(
        "rnc,ch->hrn", normed, w_bias.astype(jnp.bfloat16), preferred_element_type=jnp.float32
    ).astype(jnp.bfloat16)
    return (normed, projected, bias_rows)


def attend(projected, bias_all):
    channels = projected.shape[-1] // 4
    num_heads = bias_all.shape[0]
    head_size = channels // num_heads
    row_count, length = (projected.shape[0], projected.shape[1])
    shape_heads = (row_count, length, num_heads, head_size)
    queries = (
        (projected[..., :channels] * head_size ** (-0.5)).astype(jnp.bfloat16).reshape(shape_heads)
    )
    key_rows = projected[..., channels : 2 * channels].astype(jnp.bfloat16).reshape(shape_heads)
    value_rows = (
        projected[..., 2 * channels : 3 * channels].astype(jnp.bfloat16).reshape(shape_heads)
    )
    gate_vals = jax.nn.sigmoid(projected[..., 3 * channels :])
    scores = (
        jnp.einsum("bqhd,bkhd->bhqk", queries, key_rows, preferred_element_type=jnp.float32)
        + bias_all[None]
    )
    row_max = jnp.max(scores, axis=-1, keepdims=True)
    exp_scores = jnp.exp(scores - row_max)
    soft_weights = (exp_scores / jnp.sum(exp_scores, axis=-1, keepdims=True)).astype(jnp.bfloat16)
    mixture = jnp.einsum(
        "bhqk,bkhd->bqhd", soft_weights, value_rows, preferred_element_type=jnp.float32
    )
    return (mixture.reshape(row_count, length, channels) * gate_vals).astype(jnp.bfloat16)


def blocked(array):
    return array.reshape((array.shape[0] // 2, 2) + array.shape[1:])


def unblocked(array):
    return array.reshape((array.shape[0] * 2,) + array.shape[2:])


def gather_bias(bias_rows):
    return lax.all_gather(bias_rows, "dap", axis=1, tiled=True).astype(jnp.float32)


def to_columns(pieces):
    moved = jax.tree.map(
        lambda part, own: part.astype(own.dtype),
        lax.all_to_all(as_sent(pieces), "dap", split_axis=1, concat_axis=0, tiled=True),
        pieces,
    )
    return tuple((jnp.swapaxes(piece_moved, 0, 1) for piece_moved in moved))


def layer_backward(pair_rows, grad_in, normed, projected, bias_all, gain, w_project, w_bias, w_out):
    grad_f = grad_in.astype(jnp.float32)
    d_mixture = jnp.einsum(
        "rnd,cd->rnc", grad_in, w_out.astype(jnp.bfloat16), preferred_element_type=jnp.float32
    ).astype(jnp.bfloat16)

    def step(carry, inputs):
        proj_block, dmix_block = inputs
        mixture_block, pullback = jax.vjp(attend, proj_block, bias_all)
        d_proj_block, d_bias_block = pullback(dmix_block)
        return (carry + d_bias_block, (mixture_block, d_proj_block))

    d_bias_part, (mixture_b, d_proj_b) = lax.scan(
        step, jnp.zeros(bias_all.shape, jnp.float32), (blocked(projected), blocked(d_mixture))
    )
    mixture = unblocked(mixture_b)
    d_projected = unblocked(d_proj_b).astype(jnp.bfloat16)
    d_bias = lax.psum_scatter(d_bias_part, "dap", scatter_dimension=1, tiled=True).astype(
        jnp.bfloat16
    )
    grad_out = jnp.einsum("rnc,rnd->cd", mixture, grad_in, preferred_element_type=jnp.float32)
    grad_project = jnp.einsum(
        "rnc,rnf->cf", normed, d_projected, preferred_element_type=jnp.float32
    )
    grad_bias = jnp.einsum("rnc,hrn->ch", normed, d_bias, preferred_element_type=jnp.float32)
    d_normed = jnp.einsum(
        "rnf,cf->rnc",
        d_projected,
        w_project.astype(jnp.bfloat16),
        preferred_element_type=jnp.float32,
    )
    d_normed = d_normed + jnp.einsum(
        "hrn,ch->rnc", d_bias, w_bias.astype(jnp.bfloat16), preferred_element_type=jnp.float32
    )
    unused, norm_pull = jax.vjp(normalize, pair_rows.astype(jnp.float32), gain)
    d_input, grad_gain = norm_pull(d_normed)
    d_rows = (grad_f + d_input).astype(jnp.bfloat16)
    return (d_rows, (grad_gain, grad_project, grad_bias, grad_out))


def per_device(pair_rep, cotangent, norm_gain, w_project, w_bias, w_out):
    normed_one, proj_one, bias_one = project(pair_rep, norm_gain[0], w_project[0], w_bias[0])
    bias_all_one = gather_bias(bias_one)
    mixture_one = unblocked(
        lax.map(lambda one_block: attend(one_block, bias_all_one), blocked(proj_one))
    )
    out_one = jnp.einsum(
        "rnc,cd->rnd",
        mixture_one,
        w_out[0].astype(jnp.bfloat16),
        preferred_element_type=jnp.float32,
    )
    middle = (pair_rep.astype(jnp.float32) + out_one).astype(jnp.bfloat16)
    mid_cols, cot_cols = to_columns((middle, cotangent))
    normed_two, proj_two, bias_two = project(mid_cols, norm_gain[1], w_project[1], w_bias[1])
    bias_all_two = gather_bias(bias_two)
    d_mid_cols, grads_two = layer_backward(
        mid_cols,
        cot_cols,
        normed_two,
        proj_two,
        bias_all_two,
        norm_gain[1],
        w_project[1],
        w_bias[1],
        w_out[1],
    )
    (d_middle,) = to_columns((d_mid_cols,))
    d_pair, grads_one = layer_backward(
        pair_rep,
        d_middle,
        normed_one,
        proj_one,
        bias_all_one,
        norm_gain[0],
        w_project[0],
        w_bias[0],
        w_out[0],
    )
    stacked = tuple(
        (
            jnp.stack([first_grad, second_grad])
            for first_grad, second_grad in zip(grads_one, grads_two)
        )
    )
    stacked = lax.psum(stacked, "dap")
    return (d_pair, stacked[0], stacked[1], stacked[2], stacked[3])


def solution(mesh):
    in_specs = (P(("dp", "dap"), None, None), P(("dp", "dap"), None, None), P(), P(), P(), P())
    out_specs = (
        P(("dp", "dap"), None, None),
        P("dp", None),
        P("dp", None, None),
        P("dp", None, None),
        P("dp", None, None),
    )
    return jax.shard_map(
        per_device, mesh=mesh, in_specs=in_specs, out_specs=out_specs, check_vma=False
    )
```

profile of v0, /device:TPU:1, one launch (start us, length us, event | category | flops | bytes accessed | tf_op | source)
XLA Modules:
  0.0 886.1 jit_solution(6006253627938598607)
XLA Ops:
  8.5 1.7 fusion.68
  14.2 47.4 %all_gather.6 = bf16[4,256,256]{2,0,1:T(4,128)(2,1)S(1)} all-gather(bf16[4,8,256]{2,0,1:T(4,128)(2,1)S(1)} %fusion.64), channel_id=1, replica_groups=mesh['dp'=8,'dap'=32] {'dap'}, dimensions={1}, use_global_device_ids=true | all-gather | bytes 540672 | tf_op jit(solution)/shard_map/all_gather | solution.py:71
  61.9 2.7 fusion.81
  65.4 15.8 %while.40 = (s32[]{:T(128)}, bf16[4,2,256,128]{2,3,1,0:T(8,128)(2,1)}, f32[4,2,256,512]{2,3,1,0:T(8,128)}, f32[4,256,256]{1,2,0:T(8,128)S(1)}, s32[]{:T(128)}) while((s32[]{:T(128)}, bf16[4,2,256,128]{2,3,1,0:T(8,128)(2,1)}, f32[4,2,256,512]{2,3,1,0:T(8,128)}, f32[4,256,256]{1,2,0:T(8,128)S(1)}, s32[]{:T(128)}) %tuple.120), condition=%wide.region_5.6_spmd, body=%wide.region_2.5_spmd.sunk | while | flops 105056768 | bytes 7225921 | solution.py:127
  81.3 1.4 fusion.61
  83.8 3.7 all-to-all-start.1
  90.1 14.0 %all-to-all-done.1 = bf16[8,256,128]{2,0,1:T(8,128)(2,1)S(1)} async-done(((bf16[8,256,128]{2,0,1:T(8,128)(2,1)}), bf16[8,256,128]{2,0,1:T(8,128)(2,1)S(1)}, u32[]{:S(2)}, u32[]{:S(2)}) %all-to-all-start.1) | async-done | bytes 524320 | tf_op jit(solution)/shard_map/all_to_all | solution.py:77
  104.1 4.1 all-to-all-start
  110.3 47.7 %all_gather.7 = bf16[4,256,256]{2,0,1:T(4,128)(2,1)} all-gather(bf16[4,8,256]{2,0,1:T(4,128)(2,1)S(1)} %fusion.65), channel_id=1, replica_groups=mesh['dp'=8,'dap'=32] {'dap'}, dimensions={1}, use_global_device_ids=true | all-gather | bytes 540672 | tf_op jit(solution)/shard_map/all_gather | solution.py:71
  158.1 1.4 copy.102
  159.6 2.7 fusion.79
  163.4 1.5 broadcast.161.clone
  165.8 56.6 %while.41 = (s32[]{:T(128)}, f32[4,256,256]{1,2,0:T(8,128)}, bf16[4,2,256,128]{2,3,1,0:T(8,128)(2,1)}, bf16[4,2,256,512]{2,3,1,0:T(8,128)(2,1)}, bf16[4,2,256,12...) while((s32[]{:T(128)}, f32[4,256,256]{1,2,0:T(8,128)}, ...), condition=%wide.region_15.16_spmd.clone, body=%wide.region_8.15_spmd.clone.sunk | while | flops 220332032 | bytes 59024040 | solution.py:95
  165.8 2.2 fusion.230
  175.5 1.4 copy-done.6
  179.0 2.2 fusion.230
  188.7 1.4 copy-done.6
  191.1 2.3 select_add_fusion.16
  193.4 2.2 fusion.230
  203.1 1.4 copy-done.6
  205.6 2.3 select_add_fusion.16
  207.9 2.2 fusion.230
  217.6 1.4 copy-done.6
  220.0 2.3 select_add_fusion.16
  222.3 2.7 copy.104
  225.0 139.5 %all-reduce.17 = bf16[4,256,256]{2,0,1:T(4,128)(2,1)} all-reduce(f32[4,256,256]{2,0,1:T(4,128)} %copy.104), channel_id=2, replica_groups=mesh['dp'=8,'dap'=32] {'dap'}, use_global_device_ids=true, to_apply=%region_16.17.clone | all-reduce | flops 262144 | bytes 1572864
  365.6 1.7 multiply_reduce_fusion.1
  367.4 1.9 multiply_reduce_fusion
  371.6 9.9 %all-to-all-start.2 = ((bf16[8,256,128]{2,0,1:T(8,128)(2,1)}), bf16[8,256,128]{2,0,1:T(8,128)(2,1)S(1)}, u32[]{:S(2)}, u32[]{:S(2)}) async-start(bf16[8,256,128]{2,0,1:T(8,128)(2,1)} %copy.107), calls=%async_computation.2 | async-start | bytes 1048576 | tf_op jit(solution)/shard_map/all_to_all | solution.py:77
  381.8 1.5 convolution_bitcast_fusion.4
  383.3 1.5 convolution_bitcast_fusion.2
  384.9 3.1 convolution_bitcast_fusion
  388.0 10.1 %all-to-all-done.2 = bf16[8,256,128]{2,0,1:T(8,128)(2,1)S(1)} async-done(((bf16[8,256,128]{2,0,1:T(8,128)(2,1)}), bf16[8,256,128]{2,0,1:T(8,128)(2,1)S(1)}, u32[]{:S(2)}, u32[]{:S(2)}) %all-to-all-start.2) | async-done | bytes 524320 | tf_op jit(solution)/shard_map/all_to_all | solution.py:77
  399.2 1.5 broadcast.161
  401.5 49.5 %while.42 = (s32[]{:T(128)}, f32[4,256,256]{1,2,0:T(8,128)S(1)}, bf16[4,2,256,128]{2,3,1,0:T(8,128)(2,1)}, bf16[4,2,256,512]{2,3,1,0:T(8,128)(2,1)}, bf16[4,2,25...) while((s32[]{:T(128)}, f32[4,256,256]{1,2,0:T(8,128)S(1)}, ...), condition=%wide.region_26.27_spmd.clone, body=%wide.region_19.26_spmd.clone.sunk | while | flops 220332032 | bytes 59024040 | solution.py:95
  401.5 2.2 fusion.250
  413.8 2.2 fusion.250
  426.2 2.2 fusion.250
  438.6 2.2 fusion.250
  451.0 2.7 convolution_bitcast_fusion.1
  453.8 1.7 fusion.83
  457.2 140.3 %all-reduce.18 = bf16[4,256,256]{2,0,1:T(4,128)(2,1)S(1)} all-reduce(f32[4,256,256]{2,0,1:T(4,128)} %copy.113), channel_id=3, replica_groups=mesh['dp'=8,'dap'=32] {'dap'}, use_global_device_ids=true, to_apply=%region_27.28.clone | all-reduce | flops 262144 | bytes 1572864
  598.3 2.1 fusion.69
  603.4 74.7 %all-reduce.10 = (f32[2,128]{1,0:T(2,128)}, f32[2,128,4]{1,2,0:T(4,128)}) all-reduce(f32[2,128]{1,0:T(2,128)S(1)} %pad_maximum_fusion.3, f32[2,128,4]{1,2,0:T(4,128)S(1)} %pad_maximum_fusion.2), channel_id=1, replica_groups=mesh['dp'=8,'dap'=32] {'dap'}, use_global_device_ids=true, to_apply=%region_32.33 | all-reduce | flops 1280 | bytes 10240 | tf_op jit(solution)/shard_map/psum | solution.py:168
  678.1 1.9 add_convert_fusion
  680.1 195.7 %all-reduce.16.cloned.1.call-done = (f32[2,128,512]{2,1,0:T(8,128)}, f32[2,128,128]{2,1,0:T(8,128)}) async-done(((f32[2,128,512]{2,1,0:T(8,128)}, f32[2,128,128]{2,1,0:T(8,128)}), (f32[2,128,512]{2,1,0:T(8,128)}, f32[2,128,128]{2,1,0:T(8,128)})) %all-reduce.16.cloned.1.call-update) | async-done | bytes 655376 | tf_op jit(solution)/shard_map/psum | solution.py:168
  875.8 1.9 copy.233
  877.7 1.6 copy.234
  (339 shorter events, 115.5 us)
Async XLA Ops:
  7.2 6.2 copy-start
  8.5 5.4 copy-start.26
  10.2 3.7 copy-start.32
  10.2 3.7 copy-start.30
  11.5 2.5 copy-start.39
  12.6 147.0 %copy-start.20 = (bf16[2,128,512]{2,1,0:T(8,128)(2,1)}, bf16[2,128,512]{2,1,0:T(8,128)(2,1)S(1)}, u32[]{:S(2)}) copy-start(bf16[2,128,512]{2,1,0:T(8,128)(2,1)S(1)} %convert.46) | copy-start | bytes 786436
  14.0 50.6 %copy-start.10 = (bf16[8,256,128]{2,1,0:T(8,128)(2,1)}, bf16[8,256,128]{2,1,0:T(8,128)(2,1)S(1)}, u32[]{:S(2)}) copy-start(bf16[8,256,128]{2,1,0:T(8,128)(2,1)S(1)} %fusion.66) | copy-start | bytes 1572868
  81.3 6.3 copy-start.25
  81.3 7.5 copy-start.46
  83.8 20.3 %all-to-all-start.1 = ((bf16[8,256,128]{2,0,1:T(8,128)(2,1)}), bf16[8,256,128]{2,0,1:T(8,128)(2,1)S(1)}, u32[]{:S(2)}, u32[]{:S(2)}) async-start(bf16[8,256,128]{2,0,1:T(8,128)(2,1)} %copy.98), calls=%async_computation.1 | async-start | bytes 1048576 | tf_op jit(solution)/shard_map/all_to_all | solution.py:77
  104.1 5.2 copy-start.14
  104.1 58.2 %all-to-all-start = ((bf16[8,256,128]{2,0,1:T(8,128)(2,1)}), bf16[8,256,128]{2,0,1:T(8,128)(2,1)S(1)}, u32[]{:S(2)}, u32[]{:S(2)}) async-start(bf16[8,256,128]{2,0,1:T(8,128)(2,1)} %copy.93), calls=%async_computation | async-start | bytes 1048576 | tf_op jit(solution)/shard_map/all_to_all | solution.py:77
  108.2 1.9 copy-start.37
  108.3 2.0 copy-start.8
  109.3 50.2 %copy-start.34 = (f32[8,256]{1,0:T(8,128)}, f32[8,256]{1,0:T(8,128)S(1)}, u32[]{:S(2)}) copy-start(f32[8,256]{1,0:T(8,128)S(1)} %multiply_reduce_fusion.2) | copy-start | bytes 24580
  110.1 52.2 %copy-start.12 = (bf16[8,256,128]{2,1,0:T(8,128)(2,1)}, bf16[8,256,128]{2,1,0:T(8,128)(2,1)S(1)}, u32[]{:S(2)}) copy-start(bf16[8,256,128]{2,1,0:T(8,128)(2,1)S(1)} %multiply_convert_fusion) | copy-start | bytes 1572868
  159.5 2.7 copy-start.28
  162.3 3.5 copy-start.18
  173.8 1.6 copy-start.5
  187.0 1.6 copy-start.5
  201.5 1.6 copy-start.5
  215.9 1.6 copy-start.5
  222.3 142.2 %copy-start.7 = (bf16[4,2,256,512]{2,3,1,0:T(8,128)(2,1)S(1)}, bf16[4,2,256,512]{2,3,1,0:T(8,128)(2,1)}, u32[]{:S(2)}) copy-start(bf16[4,2,256,512]{2,3,1,0:T(8,128)(2,1)} %get-tuple-element.106) | copy-start | bytes 6291460
  222.3 142.2 %copy-start.21 = (bf16[2,128,512]{2,1,0:T(8,128)(2,1)S(1)}, bf16[2,128,512]{2,1,0:T(8,128)(2,1)}, u32[]{:S(2)}) copy-start(bf16[2,128,512]{2,1,0:T(8,128)(2,1)} %copy-done.20) | copy-start | bytes 786436
  225.0 140.3 %copy-start.38 = (bf16[2,128,4]{1,2,0:T(4,128)(2,1)S(1)}, bf16[2,128,4]{1,2,0:T(4,128)(2,1)}, u32[]{:S(2)}) copy-start(bf16[2,128,4]{1,2,0:T(4,128)(2,1)} %copy-done.36) | copy-start | bytes 6148
  225.0 140.3 %copy-start.42 = (f32[128]{0:T(128)S(1)}, f32[128]{0:T(128)}, u32[]{:S(2)}) copy-start(f32[128]{0:T(128)} %get-tuple-element.294) | copy-start | bytes 1540
  365.6 1.7 copy-start.35
  365.6 1.7 copy-start.9
  365.6 3.6 copy-start.19
  369.2 12.6 %copy-start.13 = (bf16[8,256,128]{2,1,0:T(8,128)(2,1)S(1)}, bf16[8,256,128]{2,1,0:T(8,128)(2,1)}, u32[]{:S(2)}) copy-start(bf16[8,256,128]{2,1,0:T(8,128)(2,1)} %copy-done.12) | copy-start | bytes 1572868
  371.6 26.5 %all-to-all-start.2 = ((bf16[8,256,128]{2,0,1:T(8,128)(2,1)}), bf16[8,256,128]{2,0,1:T(8,128)(2,1)S(1)}, u32[]{:S(2)}, u32[]{:S(2)}) async-start(bf16[8,256,128]{2,0,1:T(8,128)(2,1)} %copy.107), calls=%async_computation.2 | async-start | bytes 1048576 | tf_op jit(solution)/shard_map/all_to_all | solution.py:77
  381.5 494.2 %all-reduce.16.cloned.1.call-start = ((), (), s32[]{:S(2)}) async-start(), calls=%async_computation.3 | async-start | bytes 1310720 | tf_op jit(solution)/shard_map/psum | solution.py:168
  383.3 14.7 %copy-start.29 = (f32[2,128,128]{2,1,0:T(8,128)S(1)}, f32[2,128,128]{2,1,0:T(8,128)}, u32[]{:S(2)}) copy-start(f32[2,128,128]{2,1,0:T(8,128)} %param.17) | copy-start | bytes 393220
  398.1 3.4 copy-start.16
  451.0 2.8 copy-start.4
  451.0 2.8 copy-start.22
  453.8 1.8 copy-start.17
  453.8 1.8 copy-start.23
  455.8 141.7 %copy-start.11 = (bf16[8,256,128]{2,1,0:T(8,128)(2,1)S(1)}, bf16[8,256,128]{2,1,0:T(8,128)(2,1)}, u32[]{:S(2)}) copy-start(bf16[8,256,128]{2,1,0:T(8,128)(2,1)} %copy-done.10) | copy-start | bytes 1572868
  455.8 142.5 %copy-start.1 = (bf16[8,256,128]{2,1,0:T(8,128)(2,1)S(1)}, bf16[8,256,128]{2,1,0:T(8,128)(2,1)}, u32[]{:S(2)}) copy-start(bf16[8,256,128]{2,1,0:T(8,128)(2,1)} %param.12) | copy-start | bytes 1572868
  455.9 142.4 %copy-start.27 = (f32[8,256]{1,0:T(8,128)S(1)}, f32[8,256]{1,0:T(8,128)}, u32[]{:S(2)}) copy-start(f32[8,256]{1,0:T(8,128)} %copy-done.26) | copy-start | bytes 24580
  457.2 143.2 %copy-start.33 = (f32[8,256]{1,0:T(8,128)S(1)}, f32[8,256]{1,0:T(8,128)}, u32[]{:S(2)}) copy-start(f32[8,256]{1,0:T(8,128)} %copy-done.32) | copy-start | bytes 24580
  597.5 3.7 copy-start.24
  598.3 3.7 copy-start.31
  598.3 3.7 copy-start.40
  600.4 2.9 copy-start.45
  600.5 2.9 copy-start.43
  600.5 2.9 copy-start.44
  (15 other events, 20.1 us)
Sparse Core Ops, SparseCore 0:
  602.2 273.5 all-reduce.15
where the time goes:
time: 888 us; the launch traced here: 886 us
  blocking collectives  450 us (51%)
  waiting for transfers between devices  220 us (25%)
  other arithmetic  72.3 us (8%)
  matrix products  58.8 us (7%)
  local copies, waits for them, and re-layouts  51.2 us (6%)
  starting transfers between devices  18 us (2%)
  between operations  15.4 us (2%)
    unnamed x2, blocking collectives  280 us
    psum x1, waiting for transfers between devices, per_device(): stacked = lax.psum(stacked, 'dap')  196 us
    all_gather x2, blocking collectives, gather_bias(): lax.all_gather(bias_rows, 'dap', axis=1, tiled=True).astype(jnp.float32)  95.1 us
    psum x1, blocking collectives, per_device(): stacked = lax.psum(stacked, 'dap')  74.7 us
    another operation x14, other arithmetic  24.6 us
    all_to_all x3, waiting for transfers between devices, to_columns(): lax.all_to_all(as_sent(pieces), 'dap', split_axis=1, concat_axis=0, tiled...  24.1 us
    dot_general x28, matrix products, attend(): jnp.einsum('bhqk,bkhd->bqhd', soft_weights, value_rows, preferred_element...  18.8 us
  transfers between devices with their start and end apart: 4, of which 3 were waited for; matrix products, arithmetic and copies ran while one was open for 2% of the time, Pallas kernels for 0%

commit v1 on v0

--- a/solution.py
+++ b/solution.py
@@ -1,17 +1,138 @@
 import jax
 import jax.numpy as jnp
 from jax import lax
+from jax.experimental import pallas as pl
+from jax.experimental.pallas import tpu as pltpu
 from jax.sharding import PartitionSpec as P
 
 EPS = 1e-05
-
-
-def as_sent(shard):
-
-    def short(part):
-        return part.astype(jnp.bfloat16) if part.dtype == jnp.float32 else part
-
-    return jax.tree.map(short, shard)
+MESH = pl.DeviceIdType.MESH
+DAP = 32
+
+
+def peer_of(me, step):
+    return lax.rem(me + step, DAP)
+
+
+def greet(me):
+    barrier = pltpu.get_barrier_semaphore()
+
+    def tell(step, carry):
+        pl.semaphore_signal(
+            barrier, inc=1, device_id=(lax.axis_index("dp"), peer_of(me, step)), device_id_type=MESH
+        )
+        return carry
+
+    lax.fori_loop(1, DAP, tell, 0)
+    pl.semaphore_wait(barrier, DAP - 1)
+
+
+def send(src, dst, send_sem, recv_sem, peer):
+    return pltpu.make_async_remote_copy(
+        src_ref=src,
+        dst_ref=dst,
+        send_sem=send_sem,
+        recv_sem=recv_sem,
+        device_id=(lax.axis_index("dp"), peer),
+        device_id_type=MESH,
+    )
+
+
+def exchange(me, source, into, send_sem, recv_sem):
+    def start(step, carry):
+        peer = peer_of(me, step)
+        send(source(peer), into(me), send_sem.at[peer], recv_sem.at[me], peer).start()
+        return carry
+
+    def finish(step, carry):
+        peer = peer_of(me, DAP - step)
+        send(source(peer), into(peer), send_sem.at[peer], recv_sem.at[peer], peer).wait()
+        return carry
+
+    lax.fori_loop(1, DAP, start, 0)
+    lax.fori_loop(1, DAP, finish, 0)
+
+
+def gather_kernel(x_ref, out_ref, send_sem, recv_sem):
+    me = lax.axis_index("dap")
+    greet(me)
+    out_ref[me] = x_ref[...]
+    exchange(me, lambda peer: x_ref, lambda slot: out_ref.at[slot], send_sem, recv_sem)
+
+
+def swap_kernel(x_ref, out_ref, send_sem, recv_sem):
+    me = lax.axis_index("dap")
+    greet(me)
+    out_ref[me] = x_ref[me]
+    exchange(me, lambda peer: x_ref.at[peer], lambda slot: out_ref.at[slot], send_sem, recv_sem)
+
+
+def scatter_sum_kernel(x_ref, out_ref, held, send_sem, recv_sem):
+    me = lax.axis_index("dap")
+    greet(me)
+    held[me] = x_ref[me]
+    exchange(me, lambda peer: x_ref.at[peer], lambda slot: held.at[slot], send_sem, recv_sem)
+    out_ref[...] = lax.fori_loop(
+        0, DAP, lambda slot, total: total + held[slot], jnp.zeros(out_ref.shape, jnp.float32)
+    )
+
+
+def sum_kernel(x_ref, out_ref, held, mine, send_sem, recv_sem, send_two, recv_two):
+    me = lax.axis_index("dap")
+    greet(me)
+    held[me] = x_ref[me]
+    exchange(me, lambda peer: x_ref.at[peer], lambda slot: held.at[slot], send_sem, recv_sem)
+    total = lax.fori_loop(
+        0, DAP, lambda slot, total: total + held[slot], jnp.zeros(mine.shape, jnp.float32)
+    )
+    mine[...] = total
+    out_ref[me] = total
+    exchange(me, lambda peer: mine, lambda slot: out_ref.at[slot], send_two, recv_two)
+
+
+def call(kernel, number, out, scratch, *arrays):
+    return pl.pallas_call(
+        kernel,
+        out_shape=out,
+        in_specs=[pl.BlockSpec(memory_space=pltpu.VMEM)] * len(arrays),
+        out_specs=pl.BlockSpec(memory_space=pltpu.VMEM),
+        scratch_shapes=scratch,
+        compiler_params=pltpu.CompilerParams(
+            collective_id=number, has_side_effects=True, vmem_limit_bytes=32 << 20
+        ),
+    )(*arrays)
+
+
+def sems(count):
+    return [pltpu.SemaphoreType.DMA((DAP,))] * count
+
+
+def gather(x, number):
+    return call(gather_kernel, number, jax.ShapeDtypeStruct((DAP,) + x.shape, x.dtype), sems(2), x)
+
+
+def swap(x, number):
+    return call(swap_kernel, number, jax.ShapeDtypeStruct(x.shape, x.dtype), sems(2), x)
+
+
+def scatter_sum(x, number):
+    return call(
+        scatter_sum_kernel,
+        number,
+        jax.ShapeDtypeStruct(x.shape[1:], x.dtype),
+        [pltpu.VMEM(x.shape, x.dtype)] + sems(2),
+        x,
+    )
+
+
+def sum_all(x, number):
+    return call(
+        sum_kernel,
+        number,
+        jax.ShapeDtypeStruct(x.shape, x.dtype),
+        [pltpu.VMEM(x.shape, x.dtype), pltpu.VMEM(x.shape[1:], x.dtype)] + sems(4),
+        x,
+    )
 
 
 def normalize(values_f, gain):
@@ -67,20 +188,43 @@
     return array.reshape((array.shape[0] * 2,) + array.shape[2:])
 
 
-def gather_bias(bias_rows):
-    return lax.all_gather(bias_rows, "dap", axis=1, tiled=True).astype(jnp.float32)
-
-
-def to_columns(pieces):
-    moved = jax.tree.map(
-        lambda part, own: part.astype(own.dtype),
-        lax.all_to_all(as_sent(pieces), "dap", split_axis=1, concat_axis=0, tiled=True),
-        pieces,
-    )
-    return tuple((jnp.swapaxes(piece_moved, 0, 1) for piece_moved in moved))
-
-
-def layer_backward(pair_rows, grad_in, normed, projected, bias_all, gain, w_project, w_bias, w_out):
+def gather_bias(bias_rows, number):
+    heads, rows, length = bias_rows.shape
+    parts = gather(bias_rows.reshape(heads * rows, length), number)
+    parts = parts.reshape(DAP, heads, rows, length).swapaxes(0, 1)
+    return parts.reshape(heads, DAP * rows, length).astype(jnp.float32)
+
+
+def to_columns(piece, number):
+    rows, length, channels = piece.shape
+    sent = piece.reshape(rows, DAP, rows, channels).transpose(1, 0, 2, 3)
+    got = swap(sent.reshape(DAP, rows * rows, channels), number)
+    got = got.reshape(DAP, rows, rows, channels).transpose(2, 0, 1, 3)
+    return got.reshape(rows, length, channels)
+
+
+def scatter_bias(d_bias_part, number):
+    heads, length, _ = d_bias_part.shape
+    rows = length // DAP
+    sent = d_bias_part.reshape(heads, DAP, rows, length).swapaxes(0, 1)
+    got = scatter_sum(sent.reshape(DAP, heads * rows, length), number)
+    return got.reshape(heads, rows, length).astype(jnp.bfloat16)
+
+
+def sum_grads(grads, number):
+    flat = jnp.concatenate([grad.reshape(-1) for grad in grads])
+    step = DAP * 8 * 128
+    size = -(-flat.shape[0] // step) * step
+    padded = jnp.pad(flat, (0, size - flat.shape[0])).reshape(DAP, size // DAP // 128, 128)
+    total = sum_all(padded, number).reshape(-1)
+    out, at = [], 0
+    for grad in grads:
+        out.append(total[at : at + grad.size].reshape(grad.shape))
+        at += grad.size
+    return tuple(out)
+
+
+def layer_backward(pair_rows, grad_in, normed, projected, bias_all, gain, w_project, w_bias, w_out, number):
     grad_f = grad_in.astype(jnp.float32)
     d_mixture = jnp.einsum(
         "rnd,cd->rnc", grad_in, w_out.astype(jnp.bfloat16), preferred_element_type=jnp.float32
@@ -97,9 +241,7 @@
     )
     mixture = unblocked(mixture_b)
     d_projected = unblocked(d_proj_b).astype(jnp.bfloat16)
-    d_bias = lax.psum_scatter(d_bias_part, "dap", scatter_dimension=1, tiled=True).astype(
-        jnp.bfloat16
-    )
+    d_bias = scatter_bias(d_bias_part, number)
     grad_out = jnp.einsum("rnc,rnd->cd", mixture, grad_in, preferred_element_type=jnp.float32)
     grad_project = jnp.einsum(
         "rnc,rnf->cf", normed, d_projected, preferred_element_type=jnp.float32
@@ -122,7 +264,7 @@
 
 def per_device(pair_rep, cotangent, norm_gain, w_project, w_bias, w_out):
     normed_one, proj_one, bias_one = project(pair_rep, norm_gain[0], w_project[0], w_bias[0])
-    bias_all_one = gather_bias(bias_one)
+    bias_all_one = gather_bias(bias_one, 0)
     mixture_one = unblocked(
         lax.map(lambda one_block: attend(one_block, bias_all_one), blocked(proj_one))
     )
@@ -133,9 +275,9 @@
         preferred_element_type=jnp.float32,
     )
     middle = (pair_rep.astype(jnp.float32) + out_one).astype(jnp.bfloat16)
-    mid_cols, cot_cols = to_columns((middle, cotangent))
+    mid_cols, cot_cols = (to_columns(middle, 2), to_columns(cotangent, 3))
     normed_two, proj_two, bias_two = project(mid_cols, norm_gain[1], w_project[1], w_bias[1])
-    bias_all_two = gather_bias(bias_two)
+    bias_all_two = gather_bias(bias_two, 1)
     d_mid_cols, grads_two = layer_backward(
         mid_cols,
         cot_cols,
@@ -146,8 +288,9 @@
         w_project[1],
         w_bias[1],
         w_out[1],
-    )
-    (d_middle,) = to_columns((d_mid_cols,))
+        5,
+    )
+    d_middle = to_columns(d_mid_cols, 4)
     d_pair, grads_one = layer_backward(
         pair_rep,
         d_middle,
@@ -158,6 +301,7 @@
         w_project[0],
         w_bias[0],
         w_out[0],
+        6,
     )
     stacked = tuple(
         (
@@ -165,7 +309,7 @@
             for first_grad, second_grad in zip(grads_one, grads_two)
         )
     )
-    stacked = lax.psum(stacked, "dap")
+    stacked = sum_grads(stacked, 7)
     return (d_pair, stacked[0], stacked[1], stacked[2], stacked[3])
 
 

time: 888 us -> 403 us (0.45)
  blocking collectives: 450 us -> 0 us
  waiting for transfers between devices: 220 us -> 0 us
  Pallas kernels: 0 us -> 193 us
  other arithmetic: 72.3 us -> 97.3 us
  starting transfers between devices: 18 us -> 0 us
  between operations: 15.4 us -> 1.49 us
    unnamed x2 -> x0, blocking collectives: 280 us -> none
    psum x1 -> x0, waiting for transfers between devices: 196 us -> none  [per_device(): stacked = lax.psum(stacked, 'dap')]
    pallas_call x0 -> x8, Pallas kernels: none -> 193 us  [call(): pl.pallas_call(kernel, out_shape=out, in_specs=[pl.BlockSpec(memory_space...]
    all_gather x2 -> x0, blocking collectives: 95.1 us -> none  [gather_bias(): lax.all_gather(bias_rows, 'dap', axis=1, tiled=True).astype(jnp.float32)]
    psum x1 -> x0, blocking collectives: 74.7 us -> none  [per_device(): stacked = lax.psum(stacked, 'dap')]
    all_to_all x3 -> x0, waiting for transfers between devices: 24.1 us -> none  [to_columns(): lax.all_to_all(as_sent(pieces), 'dap', split_axis=1, concat_axis=0, tiled...]
    all_to_all x3 -> x0, starting transfers between devices: 17.7 us -> none  [to_columns(): lax.all_to_all(as_sent(pieces), 'dap', split_axis=1, concat_axis=0, tiled...]
    add x8, other arithmetic: 9.35 us -> 18.5 us  [step(): return (carry + d_bias_block, (mixture_block, d_proj_block))]
  transfers between devices with their start and end apart: 4 -> 0, of which waited for: 3 -> 0; matrix products, arithmetic and copies ran while one was open for 2% -> 0% of each run, Pallas kernels for 0% -> 0%
where the time goes in v1:
time: 403 us; the launch traced here: 395 us
  Pallas kernels  193 us (48%)
  other arithmetic  97.3 us (24%)
  matrix products  56.7 us (14%)
  local copies, waits for them, and re-layouts  46 us (11%)
    pallas_call x8, Pallas kernels, call(): pl.pallas_call(kernel, out_shape=out, in_specs=[pl.BlockSpec(memory_space...  193 us
    another operation x14, other arithmetic  25.3 us
    dot_general x28, matrix products, attend(): jnp.einsum('bhqk,bkhd->bqhd', soft_weights, value_rows, preferred_element...  18.8 us
    add x8, other arithmetic, step(): return (carry + d_bias_block, (mixture_block, d_proj_block))  18.5 us
    while x32, local copies, waits for them, and re-layouts  14.1 us
    dot_general x24, matrix products, attend(): jnp.einsum('bqhd,bkhd->bhqk', queries, key_rows, preferred_element_type=j...  11.2 us
    slice x8, other arithmetic, attend(): projected[..., 2 * channels:3 * channels].astype(jnp.bfloat16)  8.93 us
    dynamic_slice x16, local copies, waits for them, and re-layouts, layer_backward(): lax.scan(step, jnp.zeros(bias_all.shape, jnp.float32), (blocked(projected...  8.22 us

profile of v1, /device:TPU:1, one launch (start us, length us, event | category | flops | bytes accessed | tf_op | source)
XLA Modules:
  0.0 395.0 jit_solution(3388712494848210596)
XLA Ops:
  2.0 1.7 fusion.69
  4.5 1.6 fusion.67
  6.3 2.7 fusion.85
  9.2 18.2 %shard_map.102 = bf16[32,32,256]{2,1,0:T(8,128)(2,1)S(1)} custom-call(bf16[32,256]{1,0:T(8,128)(2,1)S(1)} %bitcast.449), custom_call_target="tpu_custom_call" | custom-call | tf_op jit(solution)/shard_map/pallas_call | solution.py:94
  28.6 15.8 %while.40 = (s32[]{:T(128)}, bf16[4,2,256,128]{2,3,1,0:T(8,128)(2,1)}, f32[4,2,256,512]{2,3,1,0:T(8,128)}, f32[4,256,256]{1,2,0:T(8,128)S(1)}, s32[]{:T(128)}) while((s32[]{:T(128)}, bf16[4,2,256,128]{2,3,1,0:T(8,128)(2,1)}, f32[4,2,256,512]{2,3,1,0:T(8,128)}, f32[4,256,256]{1,2,0:T(8,128)S(1)}, s32[]{:T(128)}) %tuple.132), condition=%wide.region_5.6_spmd, body=%wide.region_2.5_spmd.sunk | while | flops 105056768 | bytes 7225921 | solution.py:269
  28.6 1.4 fusion.221
  32.6 1.4 fusion.221
  45.4 1.5 fusion.62
  47.1 18.6 %shard_map.103 = bf16[32,64,128]{2,1,0:T(8,128)(2,1)S(1)} custom-call(bf16[32,64,128]{2,1,0:T(8,128)(2,1)S(1)} %bitcast.447), custom_call_target="tpu_custom_call" | custom-call | tf_op jit(solution)/shard_map/pallas_call | solution.py:94
  67.8 2.7 fusion.77
  70.5 2.4 fusion.65
  73.1 18.5 %shard_map.104 = bf16[32,32,256]{2,1,0:T(8,128)(2,1)S(1)} custom-call(bf16[32,256]{1,0:T(8,128)(2,1)S(1)} %bitcast.448), custom_call_target="tpu_custom_call" | custom-call | tf_op jit(solution)/shard_map/pallas_call | solution.py:94
  92.7 1.6 copy.225
  94.4 18.5 %shard_map.101 = bf16[32,64,128]{2,1,0:T(8,128)(2,1)S(1)} custom-call(bf16[32,64,128]{2,1,0:T(8,128)(2,1)S(1)} %copy_bitcast_fusion.6.x_ref), custom_call_target="tpu_custom_call" | custom-call | tf_op jit(solution)/shard_map/pallas_call | solution.py:94
  114.0 1.5 broadcast.185.clone
  116.4 70.0 %while.41 = (s32[]{:T(128)}, f32[4,256,256]{1,2,0:T(8,128)}, bf16[4,2,256,128]{2,3,1,0:T(8,128)(2,1)}, bf16[4,2,256,512]{2,3,1,0:T(8,128)(2,1)}, bf16[4,2,256,12...) while((s32[]{:T(128)}, f32[4,256,256]{1,2,0:T(8,128)}, ...), condition=%wide.region_15.16_spmd.clone, body=%wide.region_8.15_spmd.clone.sunk | while | flops 220332032 | bytes 59024040 | solution.py:239
  116.4 2.6 fusion.236
  127.9 1.4 copy-done.9
  131.3 2.3 select_add_fusion.16
  133.7 2.6 fusion.236
  145.2 1.4 copy-done.9
  148.6 2.7 select_add_fusion.16
  151.2 2.6 fusion.236
  162.8 1.4 copy-done.9
  166.1 2.7 select_add_fusion.16
  168.8 2.6 fusion.236
  180.3 1.4 copy-done.9
  183.7 2.7 select_add_fusion.16
  186.4 1.6 copy.227
  188.1 26.7 %shard_map.105 = f32[32,256]{1,0:T(8,128)S(1)} custom-call(f32[32,32,256]{2,1,0:T(8,128)S(1)} %copy_bitcast_fusion.1.x_ref), custom_call_target="tpu_custom_call" | custom-call | tf_op jit(solution)/shard_map/pallas_call | solution.py:94
  214.8 1.7 fusion.89
  218.0 1.9 multiply_reduce_fusion.1
  220.1 2.4 multiply_reduce_fusion
  223.9 22.1 %shard_map.106 = bf16[32,64,128]{2,1,0:T(8,128)(2,1)S(1)} custom-call(bf16[32,64,128]{2,1,0:T(8,128)(2,1)S(1)} %copy_bitcast_fusion.4.x_ref), custom_call_target="tpu_custom_call" | custom-call | tf_op jit(solution)/shard_map/pallas_call | solution.py:94
  247.1 1.5 broadcast.185
  249.4 56.3 %while.42 = (s32[]{:T(128)}, f32[4,256,256]{1,2,0:T(8,128)}, bf16[4,2,256,128]{2,3,1,0:T(8,128)(2,1)}, bf16[4,2,256,512]{2,3,1,0:T(8,128)(2,1)}, bf16[4,2,256,12...) while((s32[]{:T(128)}, f32[4,256,256]{1,2,0:T(8,128)}, ...), condition=%wide.region_25.26_spmd.clone, body=%wide.region_18.25_spmd.clone.sunk | while | flops 220332032 | bytes 59024040 | solution.py:239
  249.4 2.2 fusion.256
  262.6 2.2 fusion.256
  274.6 2.3 select_add_fusion.19
  277.0 2.2 fusion.256
  289.0 2.3 select_add_fusion.19
  291.4 2.2 fusion.256
  303.4 2.3 select_add_fusion.19
  305.7 1.6 copy.239
  307.5 26.7 %shard_map.107 = f32[32,256]{1,0:T(8,128)S(1)} custom-call(f32[32,32,256]{2,1,0:T(8,128)S(1)} %copy_bitcast_fusion.x_ref), custom_call_target="tpu_custom_call" | custom-call | tf_op jit(solution)/shard_map/pallas_call | solution.py:94
  338.5 1.4 convolution_bitcast_fusion
  345.5 43.6 %shard_map.108 = f32[32,48,128]{2,1,0:T(8,128)S(1)} custom-call(f32[32,48,128]{2,1,0:T(8,128)S(1)} %bitcast.442), custom_call_target="tpu_custom_call" | custom-call | tf_op jit(solution)/shard_map/pallas_call | solution.py:94
  392.0 3.0 add_convert_fusion
  (334 shorter events, 124.7 us)
Async XLA Ops:
  0.6 93.6 %copy-start = (bf16[8,256,128]{2,1,0:T(8,128)(2,1)S(1)}, bf16[8,256,128]{2,1,0:T(8,128)(2,1)}, u32[]{:S(2)}) copy-start(bf16[8,256,128]{2,1,0:T(8,128)(2,1)} %param.13) | copy-start | bytes 1572868
  0.6 5.6 %copy-start.21 = (f32[2,128,512]{2,1,0:T(8,128)S(1)}, f32[2,128,512]{2,1,0:T(8,128)}, u32[]{:S(2)}) copy-start(f32[2,128,512]{2,1,0:T(8,128)} %param.15) | copy-start | bytes 1572868
  2.0 4.1 %copy-start.22 = (f32[8,256]{1,0:T(8,128)}, f32[8,256]{1,0:T(8,128)S(1)}, u32[]{:S(2)}) copy-start(f32[8,256]{1,0:T(8,128)S(1)} %broadcast_multiply_fusion.1) | copy-start | bytes 24580
  3.7 2.5 copy-start.26
  3.7 2.4 copy-start.24
  4.5 1.7 copy-start.34
  4.5 62.7 %copy-start.28 = (f32[128]{0:T(128)}, f32[128]{0:T(128)S(1)}, u32[]{:S(2)}) copy-start(f32[128]{0:T(128)S(1)} %get-tuple-element.350) | copy-start | bytes 1540
  6.2 2.8 copy-start.12
  6.3 2.7 copy-start.17
  6.3 2.7 copy-start.31
  47.1 20.7 %copy-start.18 = (bf16[2,128,512]{2,1,0:T(8,128)(2,1)S(1)}, bf16[2,128,512]{2,1,0:T(8,128)(2,1)}, u32[]{:S(2)}) copy-start(bf16[2,128,512]{2,1,0:T(8,128)(2,1)} %copy-done.17) | copy-start | bytes 786436
  125.9 1.9 copy-start.8
  127.9 1.4 copy-start.9
  143.2 1.9 copy-start.8
  145.2 1.4 copy-start.9
  160.7 1.9 copy-start.8
  162.8 1.4 copy-start.9
  178.3 1.9 copy-start.8
  180.3 1.4 copy-start.9
  187.9 26.9 %copy-start.10 = (bf16[4,2,256,512]{2,3,1,0:T(8,128)(2,1)S(1)}, bf16[4,2,256,512]{2,3,1,0:T(8,128)(2,1)}, u32[]{:S(2)}) copy-start(bf16[4,2,256,512]{2,3,1,0:T(8,128)(2,1)} %get-tuple-element.106) | copy-start | bytes 6291460
  187.9 26.9 %copy-start.19 = (bf16[2,128,512]{2,1,0:T(8,128)(2,1)S(1)}, bf16[2,128,512]{2,1,0:T(8,128)(2,1)}, u32[]{:S(2)}) copy-start(bf16[2,128,512]{2,1,0:T(8,128)(2,1)} %copy-done.17) | copy-start | bytes 786436
  214.8 2.1 copy-start.29
  214.8 2.1 copy-start.32
  216.8 1.2 copy-start.16
  218.0 4.5 %copy-start.2 = (f32[8,32,8,128]{3,0,2,1:T(8,128)}, f32[8,32,8,128]{3,0,2,1:T(8,128)S(1)}, u32[]{:S(2)}) copy-start(f32[8,32,8,128]{3,0,2,1:T(8,128)S(1)} %convert_bitcast_fusion) | copy-start | bytes 3145732
  220.1 2.5 copy-start.14
  257.4 1.6 copy-start.5
  259.1 1.3 copy-start.6
  270.6 1.6 copy-start.5
  272.3 1.3 copy-start.6
  285.0 1.6 copy-start.5
  286.6 1.3 copy-start.6
  299.4 1.6 copy-start.5
  301.0 1.3 copy-start.6
  307.3 27.0 %copy-start.7 = (bf16[4,2,256,512]{2,3,1,0:T(8,128)(2,1)S(1)}, bf16[4,2,256,512]{2,3,1,0:T(8,128)(2,1)}, u32[]{:S(2)}) copy-start(bf16[4,2,256,512]{2,3,1,0:T(8,128)(2,1)} %get-tuple-element.108) | copy-start | bytes 6291460
  307.3 27.0 %copy-start.20 = (bf16[2,128,512]{2,1,0:T(8,128)(2,1)S(1)}, bf16[2,128,512]{2,1,0:T(8,128)(2,1)}, u32[]{:S(2)}) copy-start(bf16[2,128,512]{2,1,0:T(8,128)(2,1)} %copy-done.17) | copy-start | bytes 786436
  307.3 28.8 %copy-start.27 = (f32[8,256]{1,0:T(8,128)S(1)}, f32[8,256]{1,0:T(8,128)}, u32[]{:S(2)}) copy-start(f32[8,256]{1,0:T(8,128)} %copy-done.26) | copy-start | bytes 24580
  307.3 29.8 %copy-start.25 = (f32[8,256]{1,0:T(8,128)S(1)}, f32[8,256]{1,0:T(8,128)}, u32[]{:S(2)}) copy-start(f32[8,256]{1,0:T(8,128)} %copy-done.24) | copy-start | bytes 24580
  307.5 27.6 %copy-start.4 = (bf16[8,256,128]{2,1,0:T(8,128)(2,1)S(1)}, bf16[8,256,128]{2,1,0:T(8,128)(2,1)}, u32[]{:S(2)}) copy-start(bf16[8,256,128]{2,1,0:T(8,128)(2,1)} %param.12) | copy-start | bytes 1572868
  307.5 27.6 %copy-start.23 = (f32[8,256]{1,0:T(8,128)S(1)}, f32[8,256]{1,0:T(8,128)}, u32[]{:S(2)}) copy-start(f32[8,256]{1,0:T(8,128)} %copy-done.22) | copy-start | bytes 24580
  307.5 27.6 %copy-start.33 = (f32[2,128,4]{1,2,0:T(4,128)S(1)}, f32[2,128,4]{1,2,0:T(4,128)}, u32[]{:S(2)}) copy-start(f32[2,128,4]{1,2,0:T(4,128)} %param.16) | copy-start | bytes 12292
  307.5 27.6 %copy-start.35 = (f32[128]{0:T(128)S(1)}, f32[128]{0:T(128)}, u32[]{:S(2)}) copy-start(f32[128]{0:T(128)} %copy-done.34) | copy-start | bytes 1540
  335.1 3.3 copy-start.3
  335.1 3.3 copy-start.11
  335.1 3.3 copy-start.30
  336.1 1.0 copy-start.15
  338.4 1.5 copy-start.13
  389.0 6.0 %copy-start.1 = (bf16[8,256,128]{2,1,0:T(8,128)(2,1)S(1)}, bf16[8,256,128]{2,1,0:T(8,128)(2,1)}, u32[]{:S(2)}) copy-start(bf16[8,256,128]{2,1,0:T(8,128)(2,1)} %param.13) | copy-start | bytes 1572868

commit v2 on v0

v2 whole, which is shorter than its diff:
```python
import jax
import jax.numpy as jnp
from jax import lax
from jax.experimental import pallas as pl
from jax.experimental.pallas import tpu as pltpu
from jax.sharding import PartitionSpec as P

EPS = 1e-05
MESH = pl.DeviceIdType.MESH
F32 = jnp.float32
BF16 = jnp.bfloat16
DAP = 32
ROWS = 8
LENGTH = 256
CHANNELS = 128
HEADS = 4
BLOCKS = 4
BLOCK = LENGTH // BLOCKS
STACK = HEADS * BLOCK
SCALE = (CHANNELS // HEADS) ** (-0.5)


def slot_of(device):
    return (
        lax.rem(lax.div(device, 2), 4) * 8 + lax.div(device, 8) * 2 + lax.rem(device, 2)
    )


def device_of(slot):
    return lax.rem(lax.div(slot, 2), 4) * 8 + lax.div(slot, 8) * 2 + lax.rem(slot, 2)


def remote(src, dst, send_sem, recv_sem, slot):
    return pltpu.make_async_remote_copy(
        src_ref=src,
        dst_ref=dst,
        send_sem=send_sem,
        recv_sem=recv_sem,
        device_id=(lax.axis_index("dp"), device_of(slot)),
        device_id_type=MESH,
    )


def loop(low, high, body):
    def step(index, carry):
        body(index)
        return carry

    lax.fori_loop(low, high, step, 0)


def dot(a, b):
    return lax.dot_general(a, b, (((1,), (0,)), ((), ())), preferred_element_type=F32)


def dot_nt(a, b):
    return lax.dot_general(a, b, (((1,), (1,)), ((), ())), preferred_element_type=F32)


def dot_tn(a, b):
    return lax.dot_general(a, b, (((0,), (0,)), ((), ())), preferred_element_type=F32)


def centre(values):
    centred = values - jnp.mean(values, axis=-1, keepdims=True)
    variance = jnp.mean(centred * centred, axis=-1, keepdims=True)
    inverse = lax.rsqrt(variance + EPS)
    return centred * inverse, inverse


def kernel(
    x_ref,
    cot_ref,
    gain_ref,
    wp_ref,
    wb_ref,
    wo_ref,
    dpair_ref,
    small_ref,
    gproj_ref,
    gout_ref,
    rows_s,
    dy_s,
    norm_s,
    q_s,
    k_s,
    v_s,
    gate_s,
    o_s,
    mix_s,
    p_s,
    dproj_s,
    dkt_s,
    dvt_s,
    wp_s,
    wo_s,
    bias_f,
    bias_all,
    bias_q,
    dm_s,
    dbias_acc,
    wide_s,
    stage_s,
    cot_send,
    cot_recv,
    mid_send,
    mid_recv,
    back_send,
    back_recv,
    db_kept,
    db_pair_send,
    db_pair_recv,
    db_send,
    db_recv,
    db_s,
    wg_send,
    wg_recv,
    wg_all,
    sg_all,
    cot_ss,
    cot_rs,
    mid_ss,
    mid_rs,
    back_ss,
    back_rs,
    bias_ss,
    bias_fs,
    bias_rs,
    pair_ss,
    pair_rs,
    db_ss,
    db_rs,
    wg_ss,
    wg_rs,
    wa_ss,
    wa_fs,
    wa_rs,
    sg_ss,
    sg_rs,
):
    me = slot_of(lax.axis_index("dap"))
    mine = lax.div(me, 2)
    core = lax.rem(me, 2)
    sibling = me + 1 - 2 * core
    first_block = lax.div(me, 8)
    barrier = pltpu.get_barrier_semaphore()

    def other(step):
        return lax.rem(me + step, DAP)

    def tell(step):
        pl.semaphore_signal(
            barrier,
            inc=1,
            device_id=(lax.axis_index("dp"), device_of(other(step))),
            device_id_type=MESH,
        )

    loop(1, DAP, tell)

    lane_head = lax.div(lax.broadcasted_iota(jnp.int32, (1, CHANNELS), 1), CHANNELS // HEADS)
    masks = [jnp.where(lane_head == head, 1.0, 0.0).astype(F32) for head in range(HEADS)]
    masks_short = [mask.astype(BF16) for mask in masks]

    def stack(block):
        return jnp.concatenate([block * mask for mask in masks_short], axis=0)

    def pick(stacked):
        out = stacked[:BLOCK] * masks[0]
        for head in range(1, HEADS):
            out = out + stacked[head * BLOCK : (head + 1) * BLOCK] * masks[head]
        return out

    def block_rows(block):
        return pl.ds(pl.multiple_of(block * BLOCK, BLOCK), BLOCK)

    def gather_start(buf, ss, rs):
        remote(buf.at[me], buf.at[me], ss.at[sibling], rs.at[me], sibling).start()

        def go(step):
            slot = other(2 * step)
            remote(buf.at[me], buf.at[me], ss.at[slot], rs.at[me], slot).start()

        loop(1, DAP // 2, go)

    def gather_finish(buf, ss, fs, rs):
        def forward(step):
            slot = other(DAP - 2 * step)
            remote(buf.at[slot], buf.at[slot], ss.at[slot], rs.at[slot], slot).wait_recv()
            remote(buf.at[slot], buf.at[slot], fs.at[slot], rs.at[slot], sibling).start()

        loop(1, DAP // 2, forward)

        def take(chip):
            slot = 2 * chip + 1 - core
            remote(buf.at[slot], buf.at[slot], ss.at[slot], rs.at[slot], slot).wait_recv()

        loop(0, DAP // 2, take)

    def gather_sent(buf, ss, fs, rs):
        remote(buf.at[me], buf.at[me], ss.at[sibling], rs.at[me], sibling).wait_send()

        def done(step):
            slot = other(2 * step)
            remote(buf.at[me], buf.at[me], ss.at[slot], rs.at[me], slot).wait_send()
            remote(buf.at[slot], buf.at[slot], fs.at[slot], rs.at[slot], sibling).wait_send()

        loop(1, DAP // 2, done)

    def swap_start(send, recv, ss, rs, slot):
        @pl.when(slot != me)
        def _():
            remote(send.at[slot], recv.at[me], ss.at[slot], rs.at[me], slot).start()

    def swap_take(send, recv, ss, rs, slot):
        @pl.when(slot != me)
        def _():
            remote(send.at[slot], recv.at[slot], ss.at[slot], rs.at[slot], slot).wait_recv()

    def swap_sent(send, recv, ss, rs):
        def done(step):
            slot = other(step)
            remote(send.at[slot], recv.at[me], ss.at[slot], rs.at[me], slot).wait_send()

        loop(1, DAP, done)

    def normalise(layer, take_row):
        def row(index):
            values = take_row(index)
            hat, _ = centre(values)
            normed = (hat * gain_ref[layer : layer + 1, :]).astype(BF16)
            norm_s[layer, index] = normed
            bias = dot_nt(wb_ref[layer].astype(BF16), normed)
            for half in range(2):
                bias_f[half, pl.ds(index, HEADS, stride=ROWS), :] = bias[
                    :HEADS, half * CHANNELS : (half + 1) * CHANNELS
                ]

        loop(0, ROWS, row)
        bias_all[layer, me] = jnp.concatenate([bias_f[0], bias_f[1]], axis=1).astype(BF16)

    def project(layer):
        def row(index):
            projected = dot(norm_s[layer, index], wp_s[layer])
            q_s[layer, index] = (projected[:, :CHANNELS] * SCALE).astype(BF16)
            k_s[layer, index] = projected[:, CHANNELS : 2 * CHANNELS].astype(BF16)
            v_s[layer, index] = projected[:, 2 * CHANNELS : 3 * CHANNELS].astype(BF16)
            gate_s[layer, index] = 1.0 / (1.0 + jnp.exp(-projected[:, 3 * CHANNELS :]))

        loop(0, ROWS, row)

    def spread_bias(layer, block):
        for part in range(8):
            piece = bias_all[layer, block * 8 + part].astype(F32)
            for head in range(HEADS):
                at = head * BLOCK + part * ROWS
                bias_q[at : at + ROWS, :] = piece[head * ROWS : (head + 1) * ROWS]

    def weights(layer, index, block):
        queries = stack(q_s[layer, index, block_rows(block), :])
        scores = dot_nt(queries, k_s[layer, index]) + bias_q[...]
        shifted = jnp.exp(scores - jnp.max(scores, axis=-1, keepdims=True))
        return queries, shifted * (1.0 / jnp.sum(shifted, axis=-1, keepdims=True))

    def mix(layer, index, block, short):
        mixed = pick(dot(short, v_s[layer, index]))
        o_s[layer, index, block_rows(block), :] = mixed
        gate = gate_s[layer, index, block_rows(block), :]
        mix_s[layer, index, block_rows(block), :] = (mixed * gate).astype(BF16)
        return mixed

    def backward(layer, load_dy):
        dkt_s[...] = jnp.zeros(dkt_s.shape, F32)
        dvt_s[...] = jnp.zeros(dvt_s.shape, F32)

        def pass_on(block):
            remote(
                db_pair_send.at[layer, block],
                db_pair_recv.at[layer, block],
                pair_ss.at[layer, block],
                pair_rs.at[layer, block],
                sibling,
            ).wait_recv()
            for z in range(4):
                total = db_kept[block, z] + db_pair_recv[layer, block, z].astype(F32)
                db_send[layer, block, z] = total.astype(BF16)
                slot = block * 8 + z * 2 + core

                @pl.when(slot != me)
                def _():
                    remote(
                        db_send.at[layer, block, z],
                        db_recv.at[layer, mine],
                        db_ss.at[layer, block * 4 + z],
                        db_rs.at[layer, mine],
                        slot,
                    ).start()

                @pl.when(slot == me)
                def _():
                    db_recv[layer, mine] = db_send[layer, block, z]

        def step_block(step):
            block = lax.rem(first_block + step, BLOCKS)
            load_dy(block)
            dy = dy_s[layer, :, block_rows(block), :].reshape(ROWS * BLOCK, CHANNELS)
            dm_s[...] = dot_nt(dy, wo_s[layer]).astype(BF16).astype(F32).reshape(dm_s.shape)
            spread_bias(layer, block)
            dbias_acc[...] = jnp.zeros(dbias_acc.shape, F32)

            def row(index):
                at = block_rows(block)
                if layer == 0:
                    queries = stack(q_s[layer, index, at, :])
                    short = p_s[index, block]
                    soft = short.astype(F32)
                    mixed = o_s[layer, index, at, :]
                else:
                    queries, soft = weights(layer, index, block)
                    short = soft.astype(BF16)
                    mixed = mix(layer, index, block, short)
                gate = gate_s[layer, index, at, :]
                dm = dm_s[index]
                d_gate = dm * mixed * gate * (1.0 - gate)
                dproj_s[index, at, 3 * CHANNELS :] = d_gate.astype(BF16)
                d_mixed = stack((dm * gate).astype(BF16))
                d_soft = dot_nt(d_mixed, v_s[layer, index]).astype(BF16).astype(F32)
                product = soft * d_soft
                d_scores = product - soft * jnp.sum(product, axis=-1, keepdims=True)
                dbias_acc[...] += d_scores
                d_short = d_scores.astype(BF16)
                d_query = pick(dot(d_short, k_s[layer, index])).astype(BF16).astype(F32)
                dproj_s[index, at, :CHANNELS] = (d_query * SCALE).astype(BF16)
                dkt_s[index] += dot_tn(queries, d_short)
                dvt_s[index] += dot_tn(d_mixed, short)

            loop(0, ROWS, row)
            for z in range(4):
                for half in range(2):
                    part = z * 2 + half
                    piece = jnp.concatenate(
                        [
                            dbias_acc[
                                head * BLOCK + part * ROWS : head * BLOCK + (part + 1) * ROWS, :
                            ]
                            for head in range(HEADS)
                        ],
                        axis=0,
                    )

                    @pl.when(core == half)
                    def _():
                        db_kept[block, z] = piece

                    @pl.when(core != half)
                    def _():
                        db_pair_send[layer, block, z] = piece.astype(BF16)

            remote(
                db_pair_send.at[layer, block],
                db_pair_recv.at[layer, block],
                pair_ss.at[layer, block],
                pair_rs.at[layer, block],
                sibling,
            ).start()

            @pl.when(step > 0)
            def _():
                pass_on(lax.rem(first_block + step + BLOCKS - 1, BLOCKS))

        loop(0, BLOCKS, step_block)
        pass_on(lax.rem(first_block + BLOCKS - 1, BLOCKS))

        wide_s[...] = jnp.zeros(wide_s.shape, F32)

        def row_grads(index):
            dproj_s[index, :, CHANNELS : 2 * CHANNELS] = dkt_s[index].T.astype(BF16)
            dproj_s[index, :, 2 * CHANNELS : 3 * CHANNELS] = dvt_s[index].T.astype(BF16)
            wide_s[:, : 4 * CHANNELS] += dot_tn(norm_s[layer, index], dproj_s[index])
            wide_s[:, 4 * CHANNELS :] += dot_tn(mix_s[layer, index], dy_s[layer, index])

        loop(0, ROWS, row_grads)

        def share(slot):
            at = pl.ds(pl.multiple_of(lax.div(slot, 2) * 8, 8), 8)
            half = lax.rem(slot, 2)

            @pl.when(half == 0)
            def _():
                wg_send[layer, slot, :, : 2 * CHANNELS] = wide_s[at, : 2 * CHANNELS]

            @pl.when(half == 1)
            def _():
                wg_send[layer, slot, :, : 2 * CHANNELS] = wide_s[at, 2 * CHANNELS : 4 * CHANNELS]

            wg_send[layer, slot, :, 2 * CHANNELS :] = wide_s[at, 4 * CHANNELS :]

        loop(0, DAP, share)
        loop(
            1,
            DAP,
            lambda step: swap_start(
                wg_send.at[layer], wg_recv.at[layer], wg_ss.at[layer], wg_rs.at[layer], other(step)
            ),
        )
        wg_recv[layer, me] = wg_send[layer, me]

    def finish_bias(layer):
        def take(chip):
            @pl.when(chip != mine)
            def _():
                remote(
                    db_send.at[layer, 0, 0],
                    db_recv.at[layer, chip],
                    db_ss.at[layer, chip],
                    db_rs.at[layer, chip],
                    sibling,
                ).wait_recv()

        loop(0, DAP // 2, take)
        total = lax.fori_loop(
            0,
            DAP // 2,
            lambda chip, total: total + db_recv[layer, chip].astype(F32),
            jnp.zeros((HEADS * ROWS, LENGTH), F32),
        )
        for half in range(2):
            db_s[half] = (
                total[:, half * CHANNELS : (half + 1) * CHANNELS].astype(BF16).astype(F32)
            )

    def input_grads(layer, emit):
        finish_bias(layer)
        zero = jnp.zeros((ROWS, CHANNELS), F32)
        weight = wb_ref[layer].astype(BF16)
        gain = gain_ref[layer : layer + 1, :]

        def head_rows(index):
            at = pl.ds(index, HEADS, stride=ROWS)
            rows = jnp.concatenate([db_s[0, at, :], db_s[1, at, :]], axis=1)
            return jnp.concatenate([rows, jnp.zeros((ROWS - HEADS, LENGTH), F32)], axis=0)

        grad_bias = lax.fori_loop(
            0,
            ROWS,
            lambda index, total: total
            + dot(head_rows(index).astype(BF16), norm_s[layer, index]),
            zero,
        )

        def row(index, total):
            d_normed = dot_nt(dproj_s[index], wp_s[layer]) + dot_tn(
                head_rows(index).astype(BF16), weight
            )
            hat, inverse = centre(rows_s[layer, index].astype(F32))
            d_hat = d_normed * gain
            d_input = inverse * (
                d_hat
                - jnp.mean(d_hat, axis=-1, keepdims=True)
                - hat * jnp.mean(d_hat * hat, axis=-1, keepdims=True)
            )
            emit(index, dy_s[layer, index].astype(F32) + d_input)
            return total + jnp.sum(d_normed * hat, axis=0, keepdims=True)

        grad_gain = lax.fori_loop(0, ROWS, row, jnp.zeros((1, CHANNELS), F32))
        sg_all[layer, me] = jnp.concatenate(
            [grad_bias[:HEADS], grad_gain, zero[: ROWS - HEADS - 1]], axis=0
        )

        def go(step):
            slot = other(step)
            remote(
                sg_all.at[layer, me],
                sg_all.at[layer, me],
                sg_ss.at[layer, slot],
                sg_rs.at[layer, me],
                slot,
            ).start()

        loop(1, DAP, go)

    def weight_sums(layer):
        loop(
            1,
            DAP,
            lambda step: swap_take(
                wg_send.at[layer],
                wg_recv.at[layer],
                wg_ss.at[layer],
                wg_rs.at[layer],
                other(DAP - step),
            ),
        )
        wg_all[layer, me] = lax.fori_loop(
            0,
            DAP,
            lambda slot, total: total + wg_recv[layer, slot],
            jnp.zeros((ROWS, 3 * CHANNELS), F32),
        )
        gather_start(wg_all.at[layer], wa_ss.at[layer], wa_rs.at[layer])

    def weight_out(layer):
        gather_finish(wg_all.at[layer], wa_ss.at[layer], wa_fs.at[layer], wa_rs.at[layer])

        def place(chip):
            at = pl.ds(pl.multiple_of(chip * 8, 8), 8)
            gproj_ref[layer, at, : 2 * CHANNELS] = wg_all[layer, 2 * chip, :, : 2 * CHANNELS]
            gproj_ref[layer, at, 2 * CHANNELS :] = wg_all[layer, 2 * chip + 1, :, : 2 * CHANNELS]
            gout_ref[layer, at, :] = wg_all[layer, 2 * chip, :, 2 * CHANNELS :]

        loop(0, DAP // 2, place)

        def take(step):
            slot = other(DAP - step)
            remote(
                sg_all.at[layer, slot],
                sg_all.at[layer, slot],
                sg_ss.at[layer, slot],
                sg_rs.at[layer, slot],
                slot,
            ).wait_recv()

        loop(1, DAP, take)
        small_ref[layer] = lax.fori_loop(
            0,
            DAP,
            lambda slot, total: total + sg_all[layer, slot],
            jnp.zeros((ROWS, CHANNELS), F32),
        )

    for layer in range(2):
        wp_s[layer] = wp_ref[layer].astype(BF16)
        wo_s[layer] = wo_ref[layer].astype(BF16)
    for y in range(4):
        for z in range(4):
            rows_s[0, :, y * 64 + z * 16 : y * 64 + z * 16 + 16, :] = x_ref[
                :, z * 64 + y * 16 : z * 64 + y * 16 + 16, :
            ]
    normalise(0, lambda index: rows_s[0, index].astype(F32))
    pl.semaphore_wait(barrier, DAP - 1)
    gather_start(bias_all.at[0], bias_ss.at[0], bias_rs.at[0])

    stage_s[...] = cot_ref[...].astype(F32).reshape(stage_s.shape)

    def stage_cot(slot):
        at = device_of(slot) * ROWS
        cot_send[slot] = jnp.concatenate(
            [
                stage_s[pl.ds(pl.multiple_of(row * LENGTH + at, ROWS), ROWS), :]
                for row in range(ROWS)
            ],
            axis=0,
        ).astype(BF16)

    loop(0, DAP, stage_cot)
    loop(1, DAP, lambda step: swap_start(cot_send, cot_recv, cot_ss, cot_rs, other(step)))
    cot_recv[me] = cot_send[me]
    project(0)
    gather_finish(bias_all.at[0], bias_ss.at[0], bias_fs.at[0], bias_rs.at[0])

    def forward_block(step):
        block = lax.rem(first_block + step, BLOCKS)
        spread_bias(0, block)

        def row(index):
            _, soft = weights(0, index, block)
            short = soft.astype(BF16)
            p_s[index, block] = short
            mix(0, index, block, short)

        loop(0, ROWS, row)
        mixture = mix_s[0, :, block_rows(block), :].reshape(ROWS * BLOCK, CHANNELS)
        term = dot(mixture, wo_s[0]).reshape(ROWS, BLOCK, CHANNELS)
        middle = rows_s[0, :, block_rows(block), :].astype(F32) + term
        for part in range(8):
            slot = block * 8 + part
            mid_send[slot] = (
                middle[:, part * ROWS : (part + 1) * ROWS, :]
                .reshape(ROWS * ROWS, CHANNELS)
                .astype(BF16)
            )
            swap_start(mid_send, mid_recv, mid_ss, mid_rs, slot)

    loop(0, BLOCKS, forward_block)
    mid_recv[me] = mid_send[me]

    loop(1, DAP, lambda step: swap_take(mid_send, mid_recv, mid_ss, mid_rs, other(DAP - step)))
    stage_s[...] = mid_recv[...].astype(F32).reshape(stage_s.shape)

    def middle_row(index):
        values = stage_s[pl.ds(index, LENGTH, stride=ROWS), :]
        rows_s[1, index] = values.astype(BF16)
        return values

    normalise(1, middle_row)
    gather_start(bias_all.at[1], bias_ss.at[1], bias_rs.at[1])
    loop(1, DAP, lambda step: swap_take(cot_send, cot_recv, cot_ss, cot_rs, other(DAP - step)))
    stage_s[...] = cot_recv[...].astype(F32).reshape(stage_s.shape)

    def cot_row(index):
        dy_s[1, index] = stage_s[pl.ds(index, LENGTH, stride=ROWS), :].astype(BF16)

    loop(0, ROWS, cot_row)
    project(1)
    gather_finish(bias_all.at[1], bias_ss.at[1], bias_fs.at[1], bias_rs.at[1])
    backward(1, lambda block: None)

    def emit_back(index, values):
        stage_s[pl.ds(index, LENGTH, stride=ROWS), :] = values

    input_grads(1, emit_back)
    back_send[...] = stage_s[...].astype(BF16).reshape(back_send.shape)
    loop(1, DAP, lambda step: swap_start(back_send, back_recv, back_ss, back_rs, other(step)))
    back_recv[me] = back_send[me]

    def load_back(block):
        for part in range(8):
            swap_take(back_send, back_recv, back_ss, back_rs, block * 8 + part)
        pieces = [
            back_recv[block * 8 + part].astype(F32).reshape(ROWS, ROWS, CHANNELS)
            for part in range(8)
        ]
        dy_s[0, :, block_rows(block), :] = jnp.concatenate(pieces, axis=1).astype(BF16)

    backward(0, load_back)
    weight_sums(1)

    def emit_pair(index, values):
        short = values.astype(BF16)
        for y in range(4):
            for z in range(4):
                dpair_ref[index, z * 64 + y * 16 : z * 64 + y * 16 + 16, :] = short[
                    y * 64 + z * 16 : y * 64 + z * 16 + 16
                ]

    input_grads(0, emit_pair)
    weight_sums(0)
    weight_out(1)
    weight_out(0)

    swap_sent(cot_send, cot_recv, cot_ss, cot_rs)
    swap_sent(mid_send, mid_recv, mid_ss, mid_rs)
    swap_sent(back_send, back_recv, back_ss, back_rs)
    for layer in range(2):
        gather_sent(bias_all.at[layer], bias_ss.at[layer], bias_fs.at[layer], bias_rs.at[layer])
        gather_sent(wg_all.at[layer], wa_ss.at[layer], wa_fs.at[layer], wa_rs.at[layer])
        swap_sent(wg_send.at[layer], wg_recv.at[layer], wg_ss.at[layer], wg_rs.at[layer])

        def small_sent(step):
            slot = other(step)
            remote(
                sg_all.at[layer, me],
                sg_all.at[layer, me],
                sg_ss.at[layer, slot],
                sg_rs.at[layer, me],
                slot,
            ).wait_send()

        loop(1, DAP, small_sent)

        def db_sent(index):
            block, z = lax.div(index, 4), lax.rem(index, 4)
            slot = block * 8 + z * 2 + core

            @pl.when(slot != me)
            def _():
                remote(
                    db_send.at[layer, block, z],
                    db_recv.at[layer, mine],
                    db_ss.at[layer, index],
                    db_rs.at[layer, mine],
                    slot,
                ).wait_send()

        loop(0, DAP // 2, db_sent)

        def pair_sent(block):
            remote(
                db_pair_send.at[layer, block],
                db_pair_recv.at[layer, block],
                pair_ss.at[layer, block],
                pair_rs.at[layer, block],
                sibling,
            ).wait_send()

        loop(0, BLOCKS, pair_sent)


def per_device(pair_rep, cotangent, norm_gain, w_project, w_bias, w_out):
    w_bias_rows = jnp.pad(jnp.swapaxes(w_bias, 1, 2), ((0, 0), (0, ROWS - HEADS), (0, 0)))
    cells = (ROWS, LENGTH, CHANNELS)
    piece = (ROWS * ROWS, CHANNELS)
    bias_piece = (HEADS * ROWS, LENGTH)
    vmem = pltpu.VMEM
    sem = pltpu.SemaphoreType.DMA
    scratch = [
        vmem((2,) + cells, BF16),
        vmem((2,) + cells, BF16),
        vmem((2,) + cells, BF16),
        vmem((2,) + cells, BF16),
        vmem((2,) + cells, BF16),
        vmem((2,) + cells, BF16),
        vmem((2,) + cells, F32),
        vmem((2,) + cells, F32),
        vmem((2,) + cells, BF16),
        vmem((ROWS, BLOCKS, STACK, LENGTH), BF16),
        vmem((ROWS, LENGTH, 4 * CHANNELS), BF16),
        vmem((ROWS, CHANNELS, LENGTH), F32),
        vmem((ROWS, CHANNELS, LENGTH), F32),
        vmem((2, CHANNELS, 4 * CHANNELS), BF16),
        vmem((2, CHANNELS, CHANNELS), BF16),
        vmem((2, HEADS * ROWS, CHANNELS), F32),
        vmem((2, DAP) + bias_piece, BF16),
        vmem((STACK, LENGTH), F32),
        vmem((ROWS, BLOCK, CHANNELS), F32),
        vmem((STACK, LENGTH), F32),
        vmem((CHANNELS, 5 * CHANNELS), F32),
        vmem((ROWS * LENGTH, CHANNELS), F32),
        vmem((DAP,) + piece, BF16),
        vmem((DAP,) + piece, BF16),
        vmem((DAP,) + piece, BF16),
        vmem((DAP,) + piece, BF16),
        vmem((DAP,) + piece, BF16),
        vmem((DAP,) + piece, BF16),
        vmem((BLOCKS, 4) + bias_piece, F32),
        vmem((2, BLOCKS, 4) + bias_piece, BF16),
        vmem((2, BLOCKS, 4) + bias_piece, BF16),
        vmem((2, BLOCKS, 4) + bias_piece, BF16),
        vmem((2, DAP // 2) + bias_piece, BF16),
        vmem((2, HEADS * ROWS, CHANNELS), F32),
        vmem((2, DAP, ROWS, 3 * CHANNELS), F32),
        vmem((2, DAP, ROWS, 3 * CHANNELS), F32),
        vmem((2, DAP, ROWS, 3 * CHANNELS), F32),
        vmem((2, DAP, ROWS, CHANNELS), F32),
        sem((DAP,)),
        sem((DAP,)),
        sem((DAP,)),
        sem((DAP,)),
        sem((DAP,)),
        sem((DAP,)),
        sem((2, DAP)),
        sem((2, DAP)),
        sem((2, DAP)),
        sem((2, BLOCKS)),
        sem((2, BLOCKS)),
        sem((2, DAP // 2)),
        sem((2, DAP // 2)),
        sem((2, DAP)),
        sem((2, DAP)),
        sem((2, DAP)),
        sem((2, DAP)),
        sem((2, DAP)),
        sem((2, DAP)),
        sem((2, DAP)),
    ]
    d_pair, small, grad_project, grad_out = pl.pallas_call(
        kernel,
        out_shape=(
            jax.ShapeDtypeStruct(cells, BF16),
            jax.ShapeDtypeStruct((2, ROWS, CHANNELS), F32),
            jax.ShapeDtypeStruct((2, CHANNELS, 4 * CHANNELS), F32),
            jax.ShapeDtypeStruct((2, CHANNELS, CHANNELS), F32),
        ),
        in_specs=[pl.BlockSpec(memory_space=pltpu.VMEM)] * 6,
        out_specs=[pl.BlockSpec(memory_space=pltpu.VMEM)] * 4,
        scratch_shapes=scratch,
        compiler_params=pltpu.CompilerParams(
            collective_id=0, has_side_effects=True, vmem_limit_bytes=56 << 20
        ),
    )(pair_rep, cotangent, norm_gain, w_project, w_bias_rows, w_out)
    grad_bias = jnp.swapaxes(small[:, :HEADS], 1, 2)
    return (d_pair, small[:, HEADS], grad_project, grad_bias, grad_out)


def solution(mesh):
    in_specs = (P(("dp", "dap"), None, None), P(("dp", "dap"), None, None), P(), P(), P(), P())
    out_specs = (
        P(("dp", "dap"), None, None),
        P("dp", None),
        P("dp", None, None),
        P("dp", None, None),
        P("dp", None, None),
    )
    return jax.shard_map(
        per_device, mesh=mesh, in_specs=in_specs, out_specs=out_specs, check_vma=False
    )
```

time: 888 us -> 176 us (0.20)
  blocking collectives: 450 us -> 0 us
  waiting for transfers between devices: 220 us -> 0 us
  Pallas kernels: 0 us -> 168 us
  other arithmetic: 72.3 us -> 0 us
  matrix products: 58.8 us -> 0 us
  local copies, waits for them, and re-layouts: 51.2 us -> 7.45 us
  starting transfers between devices: 18 us -> 0 us
  between operations: 15.4 us -> 0.64 us
    unnamed x2 -> x0, blocking collectives: 280 us -> none
    psum x1 -> x0, waiting for transfers between devices: 196 us -> none  [per_device(): stacked = lax.psum(stacked, 'dap')]
    pallas_call x0 -> x1, Pallas kernels: none -> 168 us  [per_device(): pl.pallas_call(kernel, out_shape=(jax.ShapeDtypeStruct(cells, BF16), jax....]
    all_gather x2 -> x0, blocking collectives: 95.1 us -> none  [gather_bias(): lax.all_gather(bias_rows, 'dap', axis=1, tiled=True).astype(jnp.float32)]
    psum x1 -> x0, blocking collectives: 74.7 us -> none  [per_device(): stacked = lax.psum(stacked, 'dap')]
    dot_general x69 -> x0, matrix products: 55.7 us -> none  [the longest x28 18.8 us: attend(): jnp.einsum('bhqk,bkhd->bqhd', soft_weights, value_rows, preferred_element...]
    another operation x18 -> x0, other arithmetic: 26.1 us -> none
    all_to_all x3 -> x0, waiting for transfers between devices: 24.1 us -> none  [to_columns(): lax.all_to_all(as_sent(pieces), 'dap', split_axis=1, concat_axis=0, tiled...]
  transfers between devices with their start and end apart: 4 -> 0, of which waited for: 3 -> 0; matrix products, arithmetic and copies ran while one was open for 2% -> 0% of each run, Pallas kernels for 0% -> 0%
where the time goes in v2:
time: 176 us
  Pallas kernels  168 us (95%)
  local copies, waits for them, and re-layouts  7.45 us (4%)
    pallas_call x1, Pallas kernels, per_device(): pl.pallas_call(kernel, out_shape=(jax.ShapeDtypeStruct(cells, BF16), jax....  168 us
    unnamed x7, local copies, waits for them, and re-layouts  3.61 us

profile of v2, /device:TPU:1, one launch (start us, length us, event | category | flops | bytes accessed | tf_op | source)
XLA Modules:
  0.0 175.7 jit_solution(8053515501109902137)
XLA Ops:
  0.6 1.3 pad.4.wb_ref
  1.9 167.6 %shard_map.101 = (bf16[8,256,128]{2,1,0:T(8,128)(2,1)}, f32[2,8,128]{2,1,0:T(8,128)}, f32[2,128,512]{2,1,0:T(8,128)}, f32[2,128,128]{2,1,0:T(8,128)}) custom-call(bf16[8,256,128]{2,1,0:T(8,128)(2,1)} %x_ref.1, bf16[8,256,128]{2,1,0:T(8,128)(2,1)} %cot_ref.1, f32[2,128]{1,0:T(2,128)} %gain_ref.1, f32[2,128,512]{2,1,0:T(8,128)} %wp_ref.1, ...), custom_call_target="tpu_custom_call" | custom-call | tf_op jit(solution)/shard_map/pallas_call | solution.py:756
  169.5 1.3 slice_bitcast_fusion
  170.8 1.3 slice.6
  172.1 0.0 copy-start
  172.1 1.9 %copy.14 = bf16[8,256,128]{2,1,0:T(8,128)(2,1)} copy(bf16[8,256,128]{2,1,0:T(8,128)(2,1)} %get-tuple-element.18) | data formatting | bytes 1048576
  174.0 0.0 copy-done
  174.0 0.0 copy-start.1
  174.0 0.8 copy.15
  174.8 0.2 copy-done.1
  175.0 0.7 copy.16
Async XLA Ops:
  172.1 1.9 %copy-start = (f32[2,128,512]{2,1,0:T(8,128)S(1)}, f32[2,128,512]{2,1,0:T(8,128)}, u32[]{:S(2)}) copy-start(f32[2,128,512]{2,1,0:T(8,128)} %get-tuple-element.20) | copy-start | bytes 1572868
  174.0 1.0 copy-start.1

commit v3 on v2

--- a/solution.py
+++ b/solution.py
@@ -41,12 +41,12 @@
     )
 
 
-def loop(low, high, body):
+def loop(low, high, body, unroll=1):
     def step(index, carry):
         body(index)
         return carry
 
-    lax.fori_loop(low, high, step, 0)
+    lax.fori_loop(low, high, step, 0, unroll=unroll)
 
 
 def dot(a, b):
@@ -113,7 +113,10 @@
     db_send,
     db_recv,
     db_s,
-    wg_send,
+    dn_s,
+    wg_half,
+    wg_held,
+    wg_tot,
     wg_recv,
     wg_all,
     sg_all,
@@ -130,6 +133,7 @@
     pair_rs,
     db_ss,
     db_rs,
+    wg_ps,
     wg_ss,
     wg_rs,
     wa_ss,
@@ -224,19 +228,21 @@
 
         loop(1, DAP, done)
 
-    def normalise(layer, take_row):
+    def normalise(layer, index, at, values):
+        hat, _ = centre(values)
+        norm_s[layer, index, at, :] = (hat * gain_ref[layer : layer + 1, :]).astype(BF16)
+
+    def bias_start(layer):
+        weight = wb_ref[layer].astype(BF16)
+
         def row(index):
-            values = take_row(index)
-            hat, _ = centre(values)
-            normed = (hat * gain_ref[layer : layer + 1, :]).astype(BF16)
-            norm_s[layer, index] = normed
-            bias = dot_nt(wb_ref[layer].astype(BF16), normed)
+            bias = dot_nt(weight, norm_s[layer, index])
             for half in range(2):
                 bias_f[half, pl.ds(index, HEADS, stride=ROWS), :] = bias[
                     :HEADS, half * CHANNELS : (half + 1) * CHANNELS
                 ]
 
-        loop(0, ROWS, row)
+        loop(0, ROWS, row, ROWS)
         bias_all[layer, me] = jnp.concatenate([bias_f[0], bias_f[1]], axis=1).astype(BF16)
 
     def project(layer):
@@ -247,7 +253,7 @@
             v_s[layer, index] = projected[:, 2 * CHANNELS : 3 * CHANNELS].astype(BF16)
             gate_s[layer, index] = 1.0 / (1.0 + jnp.exp(-projected[:, 3 * CHANNELS :]))
 
-        loop(0, ROWS, row)
+        loop(0, ROWS, row, ROWS)
 
     def spread_bias(layer, block):
         for part in range(8):
@@ -269,7 +275,7 @@
         mix_s[layer, index, block_rows(block), :] = (mixed * gate).astype(BF16)
         return mixed
 
-    def backward(layer, load_dy):
+    def backward(layer, load_dy, between):
         dkt_s[...] = jnp.zeros(dkt_s.shape, F32)
         dvt_s[...] = jnp.zeros(dvt_s.shape, F32)
 
@@ -303,6 +309,7 @@
         def step_block(step):
             block = lax.rem(first_block + step, BLOCKS)
             load_dy(block)
+            between(step)
             dy = dy_s[layer, :, block_rows(block), :].reshape(ROWS * BLOCK, CHANNELS)
             dm_s[...] = dot_nt(dy, wo_s[layer]).astype(BF16).astype(F32).reshape(dm_s.shape)
             spread_bias(layer, block)
@@ -334,7 +341,7 @@
                 dkt_s[index] += dot_tn(queries, d_short)
                 dvt_s[index] += dot_tn(d_mixed, short)
 
-            loop(0, ROWS, row)
+            loop(0, ROWS, row, ROWS)
             for z in range(4):
                 for half in range(2):
                     part = z * 2 + half
@@ -370,7 +377,6 @@
 
         loop(0, BLOCKS, step_block)
         pass_on(lax.rem(first_block + BLOCKS - 1, BLOCKS))
-
         wide_s[...] = jnp.zeros(wide_s.shape, F32)
 
         def row_grads(index):
@@ -379,31 +385,48 @@
             wide_s[:, : 4 * CHANNELS] += dot_tn(norm_s[layer, index], dproj_s[index])
             wide_s[:, 4 * CHANNELS :] += dot_tn(mix_s[layer, index], dy_s[layer, index])
 
-        loop(0, ROWS, row_grads)
-
-        def share(slot):
-            at = pl.ds(pl.multiple_of(lax.div(slot, 2) * 8, 8), 8)
-            half = lax.rem(slot, 2)
-
-            @pl.when(half == 0)
-            def _():
-                wg_send[layer, slot, :, : 2 * CHANNELS] = wide_s[at, : 2 * CHANNELS]
-
-            @pl.when(half == 1)
-            def _():
-                wg_send[layer, slot, :, : 2 * CHANNELS] = wide_s[at, 2 * CHANNELS : 4 * CHANNELS]
-
-            wg_send[layer, slot, :, 2 * CHANNELS :] = wide_s[at, 4 * CHANNELS :]
-
-        loop(0, DAP, share)
-        loop(
-            1,
-            DAP,
-            lambda step: swap_start(
-                wg_send.at[layer], wg_recv.at[layer], wg_ss.at[layer], wg_rs.at[layer], other(step)
-            ),
-        )
-        wg_recv[layer, me] = wg_send[layer, me]
+        loop(0, ROWS, row_grads, ROWS)
+        for half in range(2):
+            at = half * 2 * CHANNELS
+            wg_half[layer, half, :, : 2 * CHANNELS] = wide_s[:, at : at + 2 * CHANNELS]
+            wg_half[layer, half, :, 2 * CHANNELS :] = wide_s[:, 4 * CHANNELS :]
+        wg_pair(layer).start()
+
+        def main(index):
+            dn_s[index] = dot_nt(dproj_s[index], wp_s[layer])
+
+        loop(0, ROWS, main, ROWS)
+
+    def wg_pair(layer):
+        return remote(
+            wg_half.at[layer, 1 - core],
+            wg_held.at[layer],
+            wg_ps.at[layer, 0],
+            wg_ps.at[layer, 1],
+            sibling,
+        )
+
+    def tile(slot):
+        return pl.ds(pl.multiple_of(lax.div(slot, 2) * ROWS, ROWS), ROWS)
+
+    def wg_copy(layer, slot, chip):
+        return remote(
+            wg_tot.at[layer, tile(slot), :],
+            wg_recv.at[layer, chip],
+            wg_ss.at[layer, lax.div(slot, 2)],
+            wg_rs.at[layer, chip],
+            slot,
+        )
+
+    def wg_start(layer):
+        wg_pair(layer).wait_recv()
+        wg_tot[layer] = wg_half[layer, core] + wg_held[layer]
+
+        def go(step):
+            wg_copy(layer, other(2 * step), mine).start()
+
+        loop(1, DAP // 2, go)
+        wg_recv[layer, mine] = wg_tot[layer, tile(me), :]
 
     def finish_bias(layer):
         def take(chip):
@@ -429,74 +452,69 @@
                 total[:, half * CHANNELS : (half + 1) * CHANNELS].astype(BF16).astype(F32)
             )
 
-    def input_grads(layer, emit):
+    def input_grads(layer, direction, emit, emitted):
         finish_bias(layer)
         zero = jnp.zeros((ROWS, CHANNELS), F32)
         weight = wb_ref[layer].astype(BF16)
         gain = gain_ref[layer : layer + 1, :]
 
-        def head_rows(index):
+        def add_bias(index, total):
             at = pl.ds(index, HEADS, stride=ROWS)
             rows = jnp.concatenate([db_s[0, at, :], db_s[1, at, :]], axis=1)
-            return jnp.concatenate([rows, jnp.zeros((ROWS - HEADS, LENGTH), F32)], axis=0)
-
-        grad_bias = lax.fori_loop(
-            0,
-            ROWS,
-            lambda index, total: total
-            + dot(head_rows(index).astype(BF16), norm_s[layer, index]),
-            zero,
-        )
-
-        def row(index, total):
-            d_normed = dot_nt(dproj_s[index], wp_s[layer]) + dot_tn(
-                head_rows(index).astype(BF16), weight
-            )
-            hat, inverse = centre(rows_s[layer, index].astype(F32))
-            d_hat = d_normed * gain
-            d_input = inverse * (
-                d_hat
-                - jnp.mean(d_hat, axis=-1, keepdims=True)
-                - hat * jnp.mean(d_hat * hat, axis=-1, keepdims=True)
-            )
-            emit(index, dy_s[layer, index].astype(F32) + d_input)
-            return total + jnp.sum(d_normed * hat, axis=0, keepdims=True)
-
-        grad_gain = lax.fori_loop(0, ROWS, row, jnp.zeros((1, CHANNELS), F32))
+            rows = jnp.concatenate([rows, jnp.zeros((ROWS - HEADS, LENGTH), F32)], axis=0)
+            rows = rows.astype(BF16)
+            dn_s[index] += dot_tn(rows, weight)
+            return total + dot(rows, norm_s[layer, index])
+
+        grad_bias = lax.fori_loop(0, ROWS, add_bias, zero, unroll=ROWS)
+
+        def step_block(step, total):
+            block = lax.rem(first_block + direction * step, BLOCKS)
+            at = block_rows(block)
+
+            def row(index, total):
+                d_normed = dn_s[index, at, :]
+                hat, inverse = centre(rows_s[layer, index, at, :].astype(F32))
+                d_hat = d_normed * gain
+                d_input = inverse * (
+                    d_hat
+                    - jnp.mean(d_hat, axis=-1, keepdims=True)
+                    - hat * jnp.mean(d_hat * hat, axis=-1, keepdims=True)
+                )
+                emit(block, index, dy_s[layer, index, at, :].astype(F32) + d_input)
+                return total + jnp.sum(d_normed * hat, axis=0, keepdims=True)
+
+            total = lax.fori_loop(0, ROWS, row, total, unroll=ROWS)
+            emitted(block)
+            return total
+
+        grad_gain = lax.fori_loop(0, BLOCKS, step_block, jnp.zeros((1, CHANNELS), F32))
         sg_all[layer, me] = jnp.concatenate(
             [grad_bias[:HEADS], grad_gain, zero[: ROWS - HEADS - 1]], axis=0
         )
 
-        def go(step):
-            slot = other(step)
-            remote(
-                sg_all.at[layer, me],
-                sg_all.at[layer, me],
-                sg_ss.at[layer, slot],
-                sg_rs.at[layer, me],
-                slot,
-            ).start()
-
-        loop(1, DAP, go)
+    def small_copy(layer, slot, from_slot):
+        return remote(
+            sg_all.at[layer, from_slot],
+            sg_all.at[layer, from_slot],
+            sg_ss.at[layer, slot],
+            sg_rs.at[layer, from_slot],
+            slot,
+        )
+
+    def small_start(layer):
+        loop(1, DAP, lambda step: small_copy(layer, other(step), me).start())
 
     def weight_sums(layer):
-        loop(
-            1,
-            DAP,
-            lambda step: swap_take(
-                wg_send.at[layer],
-                wg_recv.at[layer],
-                wg_ss.at[layer],
-                wg_rs.at[layer],
-                other(DAP - step),
-            ),
-        )
-        wg_all[layer, me] = lax.fori_loop(
-            0,
-            DAP,
-            lambda slot, total: total + wg_recv[layer, slot],
-            jnp.zeros((ROWS, 3 * CHANNELS), F32),
-        )
+        def take(step):
+            slot = other(DAP - 2 * step)
+            wg_copy(layer, slot, lax.div(slot, 2)).wait_recv()
+
+        loop(1, DAP // 2, take)
+        total = wg_recv[layer, 0]
+        for chip in range(1, DAP // 2):
+            total = total + wg_recv[layer, chip]
+        wg_all[layer, me] = total
         gather_start(wg_all.at[layer], wa_ss.at[layer], wa_rs.at[layer])
 
     def weight_out(layer):
@@ -512,13 +530,7 @@
 
         def take(step):
             slot = other(DAP - step)
-            remote(
-                sg_all.at[layer, slot],
-                sg_all.at[layer, slot],
-                sg_ss.at[layer, slot],
-                sg_rs.at[layer, slot],
-                slot,
-            ).wait_recv()
+            small_copy(layer, slot, slot).wait_recv()
 
         loop(1, DAP, take)
         small_ref[layer] = lax.fori_loop(
@@ -536,10 +548,10 @@
             rows_s[0, :, y * 64 + z * 16 : y * 64 + z * 16 + 16, :] = x_ref[
                 :, z * 64 + y * 16 : z * 64 + y * 16 + 16, :
             ]
-    normalise(0, lambda index: rows_s[0, index].astype(F32))
-    pl.semaphore_wait(barrier, DAP - 1)
-    gather_start(bias_all.at[0], bias_ss.at[0], bias_rs.at[0])
-
+    whole = pl.ds(0, LENGTH)
+    loop(0, ROWS, lambda index: normalise(0, index, whole, rows_s[0, index].astype(F32)), ROWS)
+    bias_start(0)
+    project(0)
     stage_s[...] = cot_ref[...].astype(F32).reshape(stage_s.shape)
 
     def stage_cot(slot):
@@ -552,10 +564,20 @@
             axis=0,
         ).astype(BF16)
 
-    loop(0, DAP, stage_cot)
-    loop(1, DAP, lambda step: swap_start(cot_send, cot_recv, cot_ss, cot_rs, other(step)))
+    loop(0, DAP, stage_cot, 4)
     cot_recv[me] = cot_send[me]
-    project(0)
+    pl.semaphore_wait(barrier, DAP - 1)
+    gather_start(bias_all.at[0], bias_ss.at[0], bias_rs.at[0])
+
+    def cot_start(step):
+        block = lax.rem(first_block + BLOCKS - step, BLOCKS)
+        loop(
+            0,
+            8,
+            lambda part: swap_start(cot_send, cot_recv, cot_ss, cot_rs, block * 8 + part),
+        )
+
+    cot_start(0)
     gather_finish(bias_all.at[0], bias_ss.at[0], bias_fs.at[0], bias_rs.at[0])
 
     def forward_block(step):
@@ -568,7 +590,7 @@
             p_s[index, block] = short
             mix(0, index, block, short)
 
-        loop(0, ROWS, row)
+        loop(0, ROWS, row, ROWS)
         mixture = mix_s[0, :, block_rows(block), :].reshape(ROWS * BLOCK, CHANNELS)
         term = dot(mixture, wo_s[0]).reshape(ROWS, BLOCK, CHANNELS)
         middle = rows_s[0, :, block_rows(block), :].astype(F32) + term
@@ -584,56 +606,95 @@
     loop(0, BLOCKS, forward_block)
     mid_recv[me] = mid_send[me]
 
-    loop(1, DAP, lambda step: swap_take(mid_send, mid_recv, mid_ss, mid_rs, other(DAP - step)))
-    stage_s[...] = mid_recv[...].astype(F32).reshape(stage_s.shape)
-
-    def middle_row(index):
-        values = stage_s[pl.ds(index, LENGTH, stride=ROWS), :]
-        rows_s[1, index] = values.astype(BF16)
-        return values
-
-    normalise(1, middle_row)
+    def chunk(block, index):
+        return pl.ds(block * (BLOCK * ROWS) + index, BLOCK, stride=ROWS)
+
+    def unpack(recv, block):
+        at = pl.ds(pl.multiple_of(block * (BLOCK * ROWS), BLOCK * ROWS), BLOCK * ROWS)
+        pieces = recv[pl.ds(pl.multiple_of(block * 8, 8), 8)]
+        stage_s[at, :] = pieces.astype(F32).reshape(BLOCK * ROWS, CHANNELS)
+
+    def middle_block(step):
+        block = lax.rem(first_block + BLOCKS - step, BLOCKS)
+        loop(
+            0,
+            8,
+            lambda part: swap_take(mid_send, mid_recv, mid_ss, mid_rs, block * 8 + part),
+        )
+        unpack(mid_recv, block)
+
+        def row(index):
+            values = stage_s[chunk(block, index), :]
+            rows_s[1, index, block_rows(block), :] = values.astype(BF16)
+            normalise(1, index, block_rows(block), values)
+
+        loop(0, ROWS, row, ROWS)
+
+    loop(0, BLOCKS, middle_block)
+    bias_start(1)
     gather_start(bias_all.at[1], bias_ss.at[1], bias_rs.at[1])
-    loop(1, DAP, lambda step: swap_take(cot_send, cot_recv, cot_ss, cot_rs, other(DAP - step)))
-    stage_s[...] = cot_recv[...].astype(F32).reshape(stage_s.shape)
-
-    def cot_row(index):
-        dy_s[1, index] = stage_s[pl.ds(index, LENGTH, stride=ROWS), :].astype(BF16)
-
-    loop(0, ROWS, cot_row)
     project(1)
+    loop(1, BLOCKS, cot_start)
     gather_finish(bias_all.at[1], bias_ss.at[1], bias_fs.at[1], bias_rs.at[1])
-    backward(1, lambda block: None)
-
-    def emit_back(index, values):
-        stage_s[pl.ds(index, LENGTH, stride=ROWS), :] = values
-
-    input_grads(1, emit_back)
-    back_send[...] = stage_s[...].astype(BF16).reshape(back_send.shape)
-    loop(1, DAP, lambda step: swap_start(back_send, back_recv, back_ss, back_rs, other(step)))
+
+    def load_cot(block):
+        loop(
+            0,
+            8,
+            lambda part: swap_take(cot_send, cot_recv, cot_ss, cot_rs, block * 8 + part),
+        )
+        unpack(cot_recv, block)
+        for index in range(ROWS):
+            dy_s[1, index, block_rows(block), :] = stage_s[chunk(block, index), :].astype(BF16)
+
+    backward(1, load_cot, lambda step: None)
+
+    def emit_back(block, index, values):
+        stage_s[chunk(block, index), :] = values
+
+    def back_start(block):
+        for part in range(8):
+            slot = block * 8 + part
+            at = pl.ds(pl.multiple_of(slot * (ROWS * ROWS), ROWS * ROWS), ROWS * ROWS)
+            back_send[slot] = stage_s[at, :].astype(BF16)
+            swap_start(back_send, back_recv, back_ss, back_rs, slot)
+
+    input_grads(1, BLOCKS - 1, emit_back, back_start)
     back_recv[me] = back_send[me]
 
     def load_back(block):
-        for part in range(8):
-            swap_take(back_send, back_recv, back_ss, back_rs, block * 8 + part)
+        loop(
+            0,
+            8,
+            lambda part: swap_take(back_send, back_recv, back_ss, back_rs, block * 8 + part),
+        )
         pieces = [
             back_recv[block * 8 + part].astype(F32).reshape(ROWS, ROWS, CHANNELS)
             for part in range(8)
         ]
         dy_s[0, :, block_rows(block), :] = jnp.concatenate(pieces, axis=1).astype(BF16)
 
-    backward(0, load_back)
-    weight_sums(1)
-
-    def emit_pair(index, values):
+    def sum_layer_one(step):
+        @pl.when(step == 1)
+        def _():
+            small_start(1)
+            wg_start(1)
+
+        @pl.when(step == 3)
+        def _():
+            weight_sums(1)
+
+    backward(0, load_back, sum_layer_one)
+    wg_start(0)
+
+    def emit_pair(block, index, values):
         short = values.astype(BF16)
-        for y in range(4):
-            for z in range(4):
-                dpair_ref[index, z * 64 + y * 16 : z * 64 + y * 16 + 16, :] = short[
-                    y * 64 + z * 16 : y * 64 + z * 16 + 16
-                ]
-
-    input_grads(0, emit_pair)
+        for z in range(4):
+            at = pl.ds(pl.multiple_of(z * 64 + block * 16, 16), 16)
+            dpair_ref[index, at, :] = short[z * 16 : z * 16 + 16]
+
+    input_grads(0, 1, emit_pair, lambda block: None)
+    small_start(0)
     weight_sums(0)
     weight_out(1)
     weight_out(0)
@@ -644,19 +705,9 @@
     for layer in range(2):
         gather_sent(bias_all.at[layer], bias_ss.at[layer], bias_fs.at[layer], bias_rs.at[layer])
         gather_sent(wg_all.at[layer], wa_ss.at[layer], wa_fs.at[layer], wa_rs.at[layer])
-        swap_sent(wg_send.at[layer], wg_recv.at[layer], wg_ss.at[layer], wg_rs.at[layer])
-
-        def small_sent(step):
-            slot = other(step)
-            remote(
-                sg_all.at[layer, me],
-                sg_all.at[layer, me],
-                sg_ss.at[layer, slot],
-                sg_rs.at[layer, me],
-                slot,
-            ).wait_send()
-
-        loop(1, DAP, small_sent)
+        wg_pair(layer).wait_send()
+        loop(1, DAP // 2, lambda step: wg_copy(layer, other(2 * step), mine).wait_send())
+        loop(1, DAP, lambda step: small_copy(layer, other(step), me).wait_send())
 
         def db_sent(index):
             block, z = lax.div(index, 4), lax.rem(index, 4)
@@ -728,8 +779,11 @@
         vmem((2, BLOCKS, 4) + bias_piece, BF16),
         vmem((2, DAP // 2) + bias_piece, BF16),
         vmem((2, HEADS * ROWS, CHANNELS), F32),
-        vmem((2, DAP, ROWS, 3 * CHANNELS), F32),
-        vmem((2, DAP, ROWS, 3 * CHANNELS), F32),
+        vmem(cells, F32),
+        vmem((2, 2, CHANNELS, 3 * CHANNELS), F32),
+        vmem((2, CHANNELS, 3 * CHANNELS), F32),
+        vmem((2, CHANNELS, 3 * CHANNELS), F32),
+        vmem((2, DAP // 2, ROWS, 3 * CHANNELS), F32),
         vmem((2, DAP, ROWS, 3 * CHANNELS), F32),
         vmem((2, DAP, ROWS, CHANNELS), F32),
         sem((DAP,)),
@@ -745,8 +799,9 @@
         sem((2, BLOCKS)),
         sem((2, DAP // 2)),
         sem((2, DAP // 2)),
-        sem((2, DAP)),
-        sem((2, DAP)),
+        sem((2, 2)),
+        sem((2, DAP // 2)),
+        sem((2, DAP // 2)),
         sem((2, DAP)),
         sem((2, DAP)),
         sem((2, DAP)),

time: 176 us -> 136 us (0.77)
  Pallas kernels: 168 us -> 127 us
    pallas_call x1, Pallas kernels: 168 us -> 127 us  [per_device(): pl.pallas_call(kernel, out_shape=(jax.ShapeDtypeStruct(cells, BF16), jax....]
where the time goes in v3:
time: 136 us; the launch traced here: 135 us
  Pallas kernels  127 us (93%)
  local copies, waits for them, and re-layouts  7.45 us (5%)
    pallas_call x1, Pallas kernels, per_device(): pl.pallas_call(kernel, out_shape=(jax.ShapeDtypeStruct(cells, BF16), jax....  127 us
    unnamed x7, local copies, waits for them, and re-layouts  3.61 us

profile of v3, /device:TPU:1, one launch (start us, length us, event | category | flops | bytes accessed | tf_op | source)
XLA Modules:
  0.0 135.5 jit_solution(18306741243053689210)
XLA Ops:
  0.6 1.3 pad.4.wb_ref
  1.9 127.4 %shard_map.101 = (bf16[8,256,128]{2,1,0:T(8,128)(2,1)}, f32[2,8,128]{2,1,0:T(8,128)}, f32[2,128,512]{2,1,0:T(8,128)}, f32[2,128,128]{2,1,0:T(8,128)}) custom-call(bf16[8,256,128]{2,1,0:T(8,128)(2,1)} %x_ref.1, bf16[8,256,128]{2,1,0:T(8,128)(2,1)} %cot_ref.1, f32[2,128]{1,0:T(2,128)} %gain_ref.1, f32[2,128,512]{2,1,0:T(8,128)} %wp_ref.1, ...), custom_call_target="tpu_custom_call" | custom-call | tf_op jit(solution)/shard_map/pallas_call | solution.py:811
  129.3 1.3 slice_bitcast_fusion
  130.6 1.3 slice.6
  131.9 0.0 copy-start
  131.9 1.9 %copy.14 = bf16[8,256,128]{2,1,0:T(8,128)(2,1)} copy(bf16[8,256,128]{2,1,0:T(8,128)(2,1)} %get-tuple-element.18) | data formatting | bytes 1048576
  133.8 0.0 copy-done
  133.8 0.0 copy-start.1
  133.8 0.8 copy.15
  134.6 0.2 copy-done.1
  134.8 0.7 copy.16
Async XLA Ops:
  131.9 1.9 %copy-start = (f32[2,128,512]{2,1,0:T(8,128)S(1)}, f32[2,128,512]{2,1,0:T(8,128)}, u32[]{:S(2)}) copy-start(f32[2,128,512]{2,1,0:T(8,128)} %get-tuple-element.20) | copy-start | bytes 1572868
  133.8 1.0 copy-start.1

commit v4 on v3

--- a/solution.py
+++ b/solution.py
@@ -69,6 +69,16 @@
 
 
 def kernel(
+    x_hbm,
+    cot_hbm,
+    gain_hbm,
+    wp_hbm,
+    wb_hbm,
+    wo_hbm,
+    dpair_hbm,
+    small_ref,
+    gproj_hbm,
+    gout_hbm,
     x_ref,
     cot_ref,
     gain_ref,
@@ -76,9 +86,10 @@
     wb_ref,
     wo_ref,
     dpair_ref,
-    small_ref,
     gproj_ref,
     gout_ref,
+    in_s,
+    out_s,
     rows_s,
     dy_s,
     norm_s,
@@ -94,8 +105,10 @@
     dvt_s,
     wp_s,
     wo_s,
+    wb_s,
     bias_f,
     bias_all,
+    bias_two,
     bias_q,
     dm_s,
     dbias_acc,
@@ -119,6 +132,11 @@
     wg_tot,
     wg_recv,
     wg_all,
+    wy_recv,
+    wy_tot,
+    wz_recv,
+    wg_own,
+    wg_other,
     sg_all,
     cot_ss,
     cot_rs,
@@ -127,18 +145,20 @@
     back_ss,
     back_rs,
     bias_ss,
-    bias_fs,
     bias_rs,
+    far_ss,
+    far_rs,
+    pass_ss,
+    pass_rs,
     pair_ss,
     pair_rs,
     db_ss,
     db_rs,
     wg_ps,
+    st_ss,
+    st_rs,
     wg_ss,
     wg_rs,
-    wa_ss,
-    wa_fs,
-    wa_rs,
     sg_ss,
     sg_rs,
 ):
@@ -162,6 +182,28 @@
 
     loop(1, DAP, tell)
 
+    def load(src, dst, index):
+        return pltpu.make_async_copy(src, dst, in_s.at[index])
+
+    x_load = load(x_hbm, x_ref, 0)
+    gain_load = load(gain_hbm, gain_ref, 1)
+    wb_load = load(wb_hbm, wb_ref, 2)
+    weight_loads = [load(wp_hbm, wp_ref, 3), load(wo_hbm, wo_ref, 4)]
+    cot_load = load(cot_hbm, cot_ref, 5)
+    for copy in [gain_load, wb_load, x_load] + weight_loads + [cot_load]:
+        copy.start()
+
+    def store(src, dst, index):
+        return pltpu.make_async_copy(src, dst, out_s.at[index])
+
+    pair_store = store(dpair_ref, dpair_hbm, 0)
+
+    def weight_stores(layer):
+        return [
+            store(gproj_ref.at[layer], gproj_hbm.at[layer], 1 + layer),
+            store(gout_ref.at[layer], gout_hbm.at[layer], 3 + layer),
+        ]
+
     lane_head = lax.div(lax.broadcasted_iota(jnp.int32, (1, CHANNELS), 1), CHANNELS // HEADS)
     masks = [jnp.where(lane_head == head, 1.0, 0.0).astype(F32) for head in range(HEADS)]
     masks_short = [mask.astype(BF16) for mask in masks]
@@ -178,62 +220,86 @@
     def block_rows(block):
         return pl.ds(pl.multiple_of(block * BLOCK, BLOCK), BLOCK)
 
-    def gather_start(buf, ss, rs):
-        remote(buf.at[me], buf.at[me], ss.at[sibling], rs.at[me], sibling).start()
-
-        def go(step):
-            slot = other(2 * step)
-            remote(buf.at[me], buf.at[me], ss.at[slot], rs.at[me], slot).start()
-
-        loop(1, DAP // 2, go)
-
-    def gather_finish(buf, ss, fs, rs):
-        def forward(step):
-            slot = other(DAP - 2 * step)
-            remote(buf.at[slot], buf.at[slot], ss.at[slot], rs.at[slot], slot).wait_recv()
-            remote(buf.at[slot], buf.at[slot], fs.at[slot], rs.at[slot], sibling).start()
-
-        loop(1, DAP // 2, forward)
-
-        def take(chip):
-            slot = 2 * chip + 1 - core
-            remote(buf.at[slot], buf.at[slot], ss.at[slot], rs.at[slot], slot).wait_recv()
-
-        loop(0, DAP // 2, take)
-
-    def gather_sent(buf, ss, fs, rs):
-        remote(buf.at[me], buf.at[me], ss.at[sibling], rs.at[me], sibling).wait_send()
-
-        def done(step):
-            slot = other(2 * step)
-            remote(buf.at[me], buf.at[me], ss.at[slot], rs.at[me], slot).wait_send()
-            remote(buf.at[slot], buf.at[slot], fs.at[slot], rs.at[slot], sibling).wait_send()
-
-        loop(1, DAP // 2, done)
+    def along_y(y):
+        return y * 8 + lax.rem(me, 8)
+
+    def turn(at, step):
+        return lax.rem(at + step, 4)
+
+    def near(step):
+        return first_block * 8 + lax.rem(lax.rem(me, 8) + step, 8)
+
+    def near_copy(layer, slot):
+        return remote(
+            bias_all.at[layer, me], bias_all.at[layer, me], bias_ss.at[layer], bias_rs.at[layer], slot
+        )
+
+    def near_all(layer):
+        held = bias_all.at[layer, pl.ds(0, 7)]
+        return remote(held, held, bias_ss.at[layer], bias_rs.at[layer], sibling)
+
+    def far_all(layer, ss, rs):
+        held = bias_all.at[layer, pl.ds(0, 12)]
+        return remote(held, held, ss.at[layer], rs.at[layer], sibling)
+
+    def half_of(y, half):
+        return pl.ds(pl.multiple_of(y * 8 + half * 4, 4), 4)
+
+    def far_copy(layer, y):
+        held = bias_all.at[layer, half_of(first_block, core)]
+        return remote(held, held, far_ss.at[layer], far_rs.at[layer], along_y(y))
+
+    def far_pass(layer, y):
+        held = bias_all.at[layer, half_of(y, core)]
+        return remote(held, held, pass_ss.at[layer], pass_rs.at[layer], sibling)
+
+    def near_start(layer):
+        loop(1, 8, lambda step: near_copy(layer, near(step)).start())
+
+    def far_start(layer):
+        near_all(layer).wait_recv()
+        loop(1, 4, lambda step: far_copy(layer, turn(first_block, step)).start())
+
+    def far_forward(layer):
+        far_all(layer, far_ss, far_rs).wait_recv()
+        loop(1, 4, lambda step: far_pass(layer, turn(first_block, step)).start())
+
+    def far_take(layer):
+        far_all(layer, pass_ss, pass_rs).wait_recv()
+
+    def bias_sent(layer):
+        near_all(layer).wait_send()
+        far_all(layer, far_ss, far_rs).wait_send()
+        far_all(layer, pass_ss, pass_rs).wait_send()
 
     def swap_start(send, recv, ss, rs, slot):
         @pl.when(slot != me)
         def _():
-            remote(send.at[slot], recv.at[me], ss.at[slot], rs.at[me], slot).start()
-
-    def swap_take(send, recv, ss, rs, slot):
-        @pl.when(slot != me)
-        def _():
-            remote(send.at[slot], recv.at[slot], ss.at[slot], rs.at[slot], slot).wait_recv()
-
-    def swap_sent(send, recv, ss, rs):
-        def done(step):
-            slot = other(step)
-            remote(send.at[slot], recv.at[me], ss.at[slot], rs.at[me], slot).wait_send()
-
-        loop(1, DAP, done)
+            remote(send.at[slot], recv.at[me], ss.at[0], rs.at[first_block], slot).start()
+
+    def swap_take(recv, ss, rs, block):
+        def take(count):
+            held = recv.at[pl.ds(0, count)]
+            remote(held, held, ss.at[0], rs.at[block], sibling).wait_recv()
+
+        @pl.when(block == first_block)
+        def _():
+            take(7)
+
+        @pl.when(block != first_block)
+        def _():
+            take(8)
+
+    def swap_sent(send, ss, rs):
+        held = send.at[pl.ds(0, DAP - 1)]
+        remote(held, held, ss.at[0], rs.at[0], sibling).wait_send()
 
     def normalise(layer, index, at, values):
         hat, _ = centre(values)
         norm_s[layer, index, at, :] = (hat * gain_ref[layer : layer + 1, :]).astype(BF16)
 
     def bias_start(layer):
-        weight = wb_ref[layer].astype(BF16)
+        weight = wb_s[layer].astype(BF16)
 
         def row(index):
             bias = dot_nt(weight, norm_s[layer, index])
@@ -256,6 +322,11 @@
         loop(0, ROWS, row, ROWS)
 
     def spread_bias(layer, block):
+        if layer == 1:
+            for head in range(HEADS):
+                at = head * BLOCK
+                bias_q[at : at + BLOCK, :] = bias_two[head, block_rows(block), :]
+            return
         for part in range(8):
             piece = bias_all[layer, block * 8 + part].astype(F32)
             for head in range(HEADS):
@@ -297,8 +368,8 @@
                     remote(
                         db_send.at[layer, block, z],
                         db_recv.at[layer, mine],
-                        db_ss.at[layer, block * 4 + z],
-                        db_rs.at[layer, mine],
+                        db_ss.at[layer],
+                        db_rs.at[layer],
                         slot,
                     ).start()
 
@@ -376,7 +447,6 @@
                 pass_on(lax.rem(first_block + step + BLOCKS - 1, BLOCKS))
 
         loop(0, BLOCKS, step_block)
-        pass_on(lax.rem(first_block + BLOCKS - 1, BLOCKS))
         wide_s[...] = jnp.zeros(wide_s.shape, F32)
 
         def row_grads(index):
@@ -386,6 +456,7 @@
             wide_s[:, 4 * CHANNELS :] += dot_tn(mix_s[layer, index], dy_s[layer, index])
 
         loop(0, ROWS, row_grads, ROWS)
+        pass_on(lax.rem(first_block + BLOCKS - 1, BLOCKS))
         for half in range(2):
             at = half * 2 * CHANNELS
             wg_half[layer, half, :, : 2 * CHANNELS] = wide_s[:, at : at + 2 * CHANNELS]
@@ -406,41 +477,116 @@
             sibling,
         )
 
+    def wg_add(layer):
+        wg_pair(layer).wait_recv()
+        wg_tot[layer] = wg_half[layer, core] + wg_held[layer]
+
     def tile(slot):
         return pl.ds(pl.multiple_of(lax.div(slot, 2) * ROWS, ROWS), ROWS)
 
-    def wg_copy(layer, slot, chip):
+    def wg_copy(slot):
         return remote(
-            wg_tot.at[layer, tile(slot), :],
-            wg_recv.at[layer, chip],
-            wg_ss.at[layer, lax.div(slot, 2)],
-            wg_rs.at[layer, chip],
-            slot,
+            wg_tot.at[0, tile(slot), :], wg_recv.at[mine], wg_ss.at[0], wg_rs.at[0], slot
         )
 
-    def wg_start(layer):
-        wg_pair(layer).wait_recv()
-        wg_tot[layer] = wg_half[layer, core] + wg_held[layer]
-
-        def go(step):
-            wg_copy(layer, other(2 * step), mine).start()
-
-        loop(1, DAP // 2, go)
-        wg_recv[layer, mine] = wg_tot[layer, tile(me), :]
+    def tiles_all(held, index):
+        piece = held.at[pl.ds(0, DAP // 2 - 1)]
+        return remote(piece, piece, wg_ss.at[index], wg_rs.at[index], sibling)
+
+    def wa_copy(slot):
+        held = wg_all.at[core, mine]
+        return remote(held, held, wg_ss.at[1], wg_rs.at[1], slot)
+
+    def wa_pass():
+        return remote(wg_all.at[core], wg_all.at[core], wg_ss.at[2], wg_rs.at[2], sibling)
+
+    def wg_start():
+        wg_add(0)
+        loop(1, DAP // 2, lambda step: wg_copy(other(2 * step)).start())
+        wg_recv[mine] = wg_tot[0, tile(me), :]
+
+    my_z = lax.rem(mine, 4)
+
+    def along_z(z):
+        return first_block * 8 + z * 2 + core
+
+    def quarter(y):
+        return pl.ds(pl.multiple_of(y * 32, 32), 32)
+
+    def eighth(y, z):
+        return pl.ds(pl.multiple_of(y * 32 + z * 8, 8), 8)
+
+    def stage_one(y):
+        return remote(
+            wg_tot.at[1, quarter(y), :],
+            wy_recv.at[first_block],
+            st_ss.at[0],
+            st_rs.at[0],
+            along_y(y),
+        )
+
+    def stage_two(z):
+        return remote(
+            wy_tot.at[pl.ds(pl.multiple_of(z * 8, 8), 8), :],
+            wz_recv.at[my_z],
+            st_ss.at[1],
+            st_rs.at[1],
+            along_z(z),
+        )
+
+    def stage_three(z):
+        held = wg_own.at[eighth(first_block, my_z), :]
+        return remote(held, held, st_ss.at[2], st_rs.at[2], along_z(z))
+
+    def stage_four(y):
+        held = wg_own.at[quarter(first_block), :]
+        return remote(held, held, st_ss.at[3], st_rs.at[3], along_y(y))
+
+    def stage_all(index):
+        rows = (3 * 32, 3 * 8, 3 * 8, 3 * 32)[index]
+        held = wg_own.at[pl.ds(0, rows), :]
+        return remote(held, held, st_ss.at[index], st_rs.at[index], sibling)
+
+    def stage_five():
+        return remote(wg_own, wg_other, wg_ps.at[2, 0], wg_ps.at[2, 1], sibling)
+
+    def three(copy, at):
+        loop(1, 4, lambda step: copy(turn(at, step)).start())
+
+    def sum_layer_one(step):
+        @pl.when(step == 0)
+        def _():
+            wg_add(1)
+            three(stage_one, first_block)
+            wy_recv[first_block] = wg_tot[1, quarter(first_block), :]
+
+        @pl.when(step == 1)
+        def _():
+            stage_all(0).wait_recv()
+            wy_tot[...] = wy_recv[0] + wy_recv[1] + wy_recv[2] + wy_recv[3]
+            three(stage_two, my_z)
+            wz_recv[my_z] = wy_tot[pl.ds(pl.multiple_of(my_z * 8, 8), 8), :]
+            small_start(1)
+
+        @pl.when(step == 2)
+        def _():
+            stage_all(1).wait_recv()
+            wg_own[eighth(first_block, my_z), :] = (
+                wz_recv[0] + wz_recv[1] + wz_recv[2] + wz_recv[3]
+            )
+            three(stage_three, my_z)
+
+        @pl.when(step == 3)
+        def _():
+            stage_all(2).wait_recv()
+            three(stage_four, first_block)
+
+    def db_all(layer):
+        held = db_recv.at[layer, pl.ds(0, DAP // 2 - 1)]
+        return remote(held, held, db_ss.at[layer], db_rs.at[layer], sibling)
 
     def finish_bias(layer):
-        def take(chip):
-            @pl.when(chip != mine)
-            def _():
-                remote(
-                    db_send.at[layer, 0, 0],
-                    db_recv.at[layer, chip],
-                    db_ss.at[layer, chip],
-                    db_rs.at[layer, chip],
-                    sibling,
-                ).wait_recv()
-
-        loop(0, DAP // 2, take)
+        db_all(layer).wait_recv()
         total = lax.fori_loop(
             0,
             DAP // 2,
@@ -455,7 +601,7 @@
     def input_grads(layer, direction, emit, emitted):
         finish_bias(layer)
         zero = jnp.zeros((ROWS, CHANNELS), F32)
-        weight = wb_ref[layer].astype(BF16)
+        weight = wb_s[layer].astype(BF16)
         gain = gain_ref[layer : layer + 1, :]
 
         def add_bias(index, total):
@@ -493,56 +639,65 @@
             [grad_bias[:HEADS], grad_gain, zero[: ROWS - HEADS - 1]], axis=0
         )
 
-    def small_copy(layer, slot, from_slot):
-        return remote(
-            sg_all.at[layer, from_slot],
-            sg_all.at[layer, from_slot],
-            sg_ss.at[layer, slot],
-            sg_rs.at[layer, from_slot],
-            slot,
-        )
+    def small_copy(layer, slot):
+        held = sg_all.at[layer, me]
+        return remote(held, held, sg_ss.at[layer], sg_rs.at[layer], slot)
+
+    def small_all(layer):
+        held = sg_all.at[layer, pl.ds(0, DAP - 1)]
+        return remote(held, held, sg_ss.at[layer], sg_rs.at[layer], sibling)
 
     def small_start(layer):
-        loop(1, DAP, lambda step: small_copy(layer, other(step), me).start())
-
-    def weight_sums(layer):
-        def take(step):
-            slot = other(DAP - 2 * step)
-            wg_copy(layer, slot, lax.div(slot, 2)).wait_recv()
-
-        loop(1, DAP // 2, take)
-        total = wg_recv[layer, 0]
+        loop(1, DAP, lambda step: small_copy(layer, other(step)).start())
+
+    def weight_sums():
+        tiles_all(wg_recv, 0).wait_recv()
+        total = wg_recv[0]
         for chip in range(1, DAP // 2):
-            total = total + wg_recv[layer, chip]
-        wg_all[layer, me] = total
-        gather_start(wg_all.at[layer], wa_ss.at[layer], wa_rs.at[layer])
-
-    def weight_out(layer):
-        gather_finish(wg_all.at[layer], wa_ss.at[layer], wa_fs.at[layer], wa_rs.at[layer])
+            total = total + wg_recv[chip]
+        wg_all[core, mine] = total
+        loop(1, DAP // 2, lambda step: wa_copy(other(2 * step)).start())
+
+    def small_out(layer):
+        small_all(layer).wait_recv()
+        total = sg_all[layer, 0]
+        for slot in range(1, DAP):
+            total = total + sg_all[layer, slot]
+        small_ref[layer] = total
+
+    def weight_out():
+        tiles_all(wg_all.at[core], 1).wait_recv()
+        wa_pass().start()
+        wa_pass().wait_recv()
 
         def place(chip):
             at = pl.ds(pl.multiple_of(chip * 8, 8), 8)
-            gproj_ref[layer, at, : 2 * CHANNELS] = wg_all[layer, 2 * chip, :, : 2 * CHANNELS]
-            gproj_ref[layer, at, 2 * CHANNELS :] = wg_all[layer, 2 * chip + 1, :, : 2 * CHANNELS]
-            gout_ref[layer, at, :] = wg_all[layer, 2 * chip, :, 2 * CHANNELS :]
-
-        loop(0, DAP // 2, place)
-
-        def take(step):
-            slot = other(DAP - step)
-            small_copy(layer, slot, slot).wait_recv()
-
-        loop(1, DAP, take)
-        small_ref[layer] = lax.fori_loop(
-            0,
-            DAP,
-            lambda slot, total: total + sg_all[layer, slot],
-            jnp.zeros((ROWS, CHANNELS), F32),
+            gproj_ref[0, at, : 2 * CHANNELS] = wg_all[0, chip, :, : 2 * CHANNELS]
+            gproj_ref[0, at, 2 * CHANNELS :] = wg_all[1, chip, :, : 2 * CHANNELS]
+            gout_ref[0, at, :] = wg_all[0, chip, :, 2 * CHANNELS :]
+
+        loop(0, DAP // 2, place, 4)
+
+    def weight_out_one():
+        stage_five().wait_recv()
+        gout_ref[1] = wg_own[:, 2 * CHANNELS :]
+
+        @pl.when(core == 0)
+        def _():
+            gproj_ref[1, :, : 2 * CHANNELS] = wg_own[:, : 2 * CHANNELS]
+            gproj_ref[1, :, 2 * CHANNELS :] = wg_other[:, : 2 * CHANNELS]
+
+        @pl.when(core == 1)
+        def _():
+            gproj_ref[1, :, : 2 * CHANNELS] = wg_other[:, : 2 * CHANNELS]
+            gproj_ref[1, :, 2 * CHANNELS :] = wg_own[:, : 2 * CHANNELS]
+
+    for copy in [gain_load, wb_load, x_load]:
+        copy.wait()
+    for layer in range(2):
+        wb_s[layer] = jnp.concatenate(
+            [wb_ref[layer], jnp.zeros((ROWS - HEADS, CHANNELS), F32)], axis=0
         )
-
-    for layer in range(2):
-        wp_s[layer] = wp_ref[layer].astype(BF16)
-        wo_s[layer] = wo_ref[layer].astype(BF16)
     for y in range(4):
         for z in range(4):
             rows_s[0, :, y * 64 + z * 16 : y * 64 + z * 16 + 16, :] = x_ref[
@@ -551,7 +706,13 @@
     whole = pl.ds(0, LENGTH)
     loop(0, ROWS, lambda index: normalise(0, index, whole, rows_s[0, index].astype(F32)), ROWS)
     bias_start(0)
+    for copy in weight_loads:
+        copy.wait()
+    for layer in range(2):
+        wp_s[layer] = wp_ref[layer].astype(BF16)
+        wo_s[layer] = wo_ref[layer].astype(BF16)
     project(0)
+    cot_load.wait()
     stage_s[...] = cot_ref[...].astype(F32).reshape(stage_s.shape)
 
     def stage_cot(slot):
@@ -567,7 +728,7 @@
     loop(0, DAP, stage_cot, 4)
     cot_recv[me] = cot_send[me]
     pl.semaphore_wait(barrier, DAP - 1)
-    gather_start(bias_all.at[0], bias_ss.at[0], bias_rs.at[0])
+    near_start(0)
 
     def cot_start(step):
         block = lax.rem(first_block + BLOCKS - step, BLOCKS)
@@ -577,11 +738,17 @@
             lambda part: swap_start(cot_send, cot_recv, cot_ss, cot_rs, block * 8 + part),
         )
 
-    cot_start(0)
-    gather_finish(bias_all.at[0], bias_ss.at[0], bias_fs.at[0], bias_rs.at[0])
+    far_start(0)
+    loop(0, 2, cot_start)
 
     def forward_block(step):
         block = lax.rem(first_block + step, BLOCKS)
+
+        @pl.when(step == 1)
+        def _():
+            far_forward(0)
+            far_take(0)
+
         spread_bias(0, block)
 
         def row(index):
@@ -594,6 +761,14 @@
         mixture = mix_s[0, :, block_rows(block), :].reshape(ROWS * BLOCK, CHANNELS)
         term = dot(mixture, wo_s[0]).reshape(ROWS, BLOCK, CHANNELS)
         middle = rows_s[0, :, block_rows(block), :].astype(F32) + term
+        hat, _ = centre(middle.astype(BF16).astype(F32))
+        norm_s[1, :, block_rows(block), :] = (hat * gain_ref[1:2, :]).astype(BF16)
+
+        @pl.when(step == BLOCKS - 1)
+        def _():
+            bias_start(1)
+            near_start(1)
+
         for part in range(8):
             slot = block * 8 + part
             mid_send[slot] = (
@@ -616,12 +791,12 @@
 
     def middle_block(step):
         block = lax.rem(first_block + BLOCKS - step, BLOCKS)
-        loop(
-            0,
-            8,
-            lambda part: swap_take(mid_send, mid_recv, mid_ss, mid_rs, block * 8 + part),
-        )
+        swap_take(mid_recv, mid_ss, mid_rs, block)
         unpack(mid_recv, block)
+
+        @pl.when(step == 1)
+        def _():
+            far_start(1)
 
         def row(index):
             values = stage_s[chunk(block, index), :]
@@ -631,18 +806,16 @@
         loop(0, ROWS, row, ROWS)
 
     loop(0, BLOCKS, middle_block)
-    bias_start(1)
-    gather_start(bias_all.at[1], bias_ss.at[1], bias_rs.at[1])
+    far_forward(1)
+    loop(2, BLOCKS, cot_start)
     project(1)
-    loop(1, BLOCKS, cot_start)
-    gather_finish(bias_all.at[1], bias_ss.at[1], bias_fs.at[1], bias_rs.at[1])
+    far_take(1)
+    for head in range(HEADS):
+        pieces = bias_all[1].astype(F32)[:, head * ROWS : (head + 1) * ROWS, :]
+        bias_two[head] = pieces.reshape(LENGTH, LENGTH).T
 
     def load_cot(block):
-        loop(
-            0,
-            8,
-            lambda part: swap_take(cot_send, cot_recv, cot_ss, cot_rs, block * 8 + part),
-        )
+        swap_take(cot_recv, cot_ss, cot_rs, block)
         unpack(cot_recv, block)
         for index in range(ROWS):
             dy_s[1, index, block_rows(block), :] = stage_s[chunk(block, index), :].astype(BF16)
@@ -663,29 +836,17 @@
     back_recv[me] = back_send[me]
 
     def load_back(block):
-        loop(
-            0,
-            8,
-            lambda part: swap_take(back_send, back_recv, back_ss, back_rs, block * 8 + part),
-        )
+        swap_take(back_recv, back_ss, back_rs, block)
         pieces = [
             back_recv[block * 8 + part].astype(F32).reshape(ROWS, ROWS, CHANNELS)
             for part in range(8)
         ]
         dy_s[0, :, block_rows(block), :] = jnp.concatenate(pieces, axis=1).astype(BF16)
 
-    def sum_layer_one(step):
-        @pl.when(step == 1)
-        def _():
-            small_start(1)
-            wg_start(1)
-
-        @pl.when(step == 3)
-        def _():
-            weight_sums(1)
-
     backward(0, load_back, sum_layer_one)
-    wg_start(0)
+    wg_start()
+    stage_all(3).wait_recv()
+    stage_five().start()
 
     def emit_pair(block, index, values):
         short = values.astype(BF16)
@@ -695,35 +856,34 @@
 
     input_grads(0, 1, emit_pair, lambda block: None)
     small_start(0)
-    weight_sums(0)
-    weight_out(1)
-    weight_out(0)
-
-    swap_sent(cot_send, cot_recv, cot_ss, cot_rs)
-    swap_sent(mid_send, mid_recv, mid_ss, mid_rs)
-    swap_sent(back_send, back_recv, back_ss, back_rs)
+    pair_store.start()
+    weight_sums()
+    weight_out_one()
+    for copy in weight_stores(1):
+        copy.start()
+    small_out(1)
+    small_out(0)
+    weight_out()
+    for copy in weight_stores(0):
+        copy.start()
+
+    swap_sent(cot_send, cot_ss, cot_rs)
+    swap_sent(mid_send, mid_ss, mid_rs)
+    swap_sent(back_send, back_ss, back_rs)
+    bias_sent(0)
+    bias_sent(1)
+    tiles_all(wg_recv, 0).wait_send()
+    tiles_all(wg_recv, 1).wait_send()
+    wa_pass().wait_send()
+
+    for index in range(4):
+        stage_all(index).wait_send()
+    stage_five().wait_send()
     for layer in range(2):
-        gather_sent(bias_all.at[layer], bias_ss.at[layer], bias_fs.at[layer], bias_rs.at[layer])
-        gather_sent(wg_all.at[layer], wa_ss.at[layer], wa_fs.at[layer], wa_rs.at[layer])
         wg_pair(layer).wait_send()
-        loop(1, DAP // 2, lambda step: wg_copy(layer, other(2 * step), mine).wait_send())
-        loop(1, DAP, lambda step: small_copy(layer, other(step), me).wait_send())
-
-        def db_sent(index):
-            block, z = lax.div(index, 4), lax.rem(index, 4)
-            slot = block * 8 + z * 2 + core
-
-            @pl.when(slot != me)
-            def _():
-                remote(
-                    db_send.at[layer, block, z],
-                    db_recv.at[layer, mine],
-                    db_ss.at[layer, index],
-                    db_rs.at[layer, mine],
-                    slot,
-                ).wait_send()
-
-        loop(0, DAP // 2, db_sent)
+        small_all(layer).wait_send()
+
+        db_all(layer).wait_send()
 
         def pair_sent(block):
             remote(
@@ -736,15 +896,39 @@
 
         loop(0, BLOCKS, pair_sent)
 
+    for copy in [pair_store] + weight_stores(1) + weight_stores(0):
+        copy.wait()
+
+
+def finish_kernel(
+    pair_ref, small_ref, proj_ref, out_ref, d_pair_ref, ggain_ref, gproj_ref, gbias_ref, gout_ref
+):
+    d_pair_ref[...] = pair_ref[...]
+    gproj_ref[...] = proj_ref[...]
+    gout_ref[...] = out_ref[...]
+    for layer in range(2):
+        gbias_ref[layer] = small_ref[layer, :HEADS, :]
+        ggain_ref[layer : layer + 1, :] = small_ref[layer, HEADS : HEADS + 1, :]
+
 
 def per_device(pair_rep, cotangent, norm_gain, w_project, w_bias, w_out):
-    w_bias_rows = jnp.pad(jnp.swapaxes(w_bias, 1, 2), ((0, 0), (0, ROWS - HEADS), (0, 0)))
     cells = (ROWS, LENGTH, CHANNELS)
     piece = (ROWS * ROWS, CHANNELS)
     bias_piece = (HEADS * ROWS, LENGTH)
     vmem = pltpu.VMEM
     sem = pltpu.SemaphoreType.DMA
     scratch = [
+        vmem(cells, BF16),
+        vmem(cells, BF16),
+        vmem((2, CHANNELS), F32),
+        vmem((2, CHANNELS, 4 * CHANNELS), F32),
+        vmem((2, HEADS, CHANNELS), F32),
+        vmem((2, CHANNELS, CHANNELS), F32),
+        vmem(cells, BF16),
+        vmem((2, CHANNELS, 4 * CHANNELS), F32),
+        vmem((2, CHANNELS, CHANNELS), F32),
+        sem((6,)),
+        sem((5,)),
         vmem((2,) + cells, BF16),
         vmem((2,) + cells, BF16),
         vmem((2,) + cells, BF16),
@@ -760,8 +944,10 @@
         vmem((ROWS, CHANNELS, LENGTH), F32),
         vmem((2, CHANNELS, 4 * CHANNELS), BF16),
         vmem((2, CHANNELS, CHANNELS), BF16),
+        vmem((2, ROWS, CHANNELS), F32),
         vmem((2, HEADS * ROWS, CHANNELS), F32),
         vmem((2, DAP) + bias_piece, BF16),
+        vmem((HEADS, LENGTH, LENGTH), F32),
         vmem((STACK, LENGTH), F32),
         vmem((ROWS, BLOCK, CHANNELS), F32),
         vmem((STACK, LENGTH), F32),
@@ -783,31 +969,40 @@
         vmem((2, 2, CHANNELS, 3 * CHANNELS), F32),
         vmem((2, CHANNELS, 3 * CHANNELS), F32),
         vmem((2, CHANNELS, 3 * CHANNELS), F32),
+        vmem((DAP // 2, ROWS, 3 * CHANNELS), F32),
         vmem((2, DAP // 2, ROWS, 3 * CHANNELS), F32),
-        vmem((2, DAP, ROWS, 3 * CHANNELS), F32),
+        vmem((4, 4 * ROWS, 3 * CHANNELS), F32),
+        vmem((4 * ROWS, 3 * CHANNELS), F32),
+        vmem((4, ROWS, 3 * CHANNELS), F32),
+        vmem((CHANNELS, 3 * CHANNELS), F32),
+        vmem((CHANNELS, 3 * CHANNELS), F32),
         vmem((2, DAP, ROWS, CHANNELS), F32),
-        sem((DAP,)),
-        sem((DAP,)),
-        sem((DAP,)),
-        sem((DAP,)),
-        sem((DAP,)),
-        sem((DAP,)),
-        sem((2, DAP)),
-        sem((2, DAP)),
-        sem((2, DAP)),
+        sem((1,)),
+        sem((BLOCKS,)),
+        sem((1,)),
+        sem((BLOCKS,)),
+        sem((1,)),
+        sem((BLOCKS,)),
+        sem((2,)),
+        sem((2,)),
+        sem((2,)),
+        sem((2,)),
+        sem((2,)),
+        sem((2,)),
         sem((2, BLOCKS)),
         sem((2, BLOCKS)),
-        sem((2, DAP // 2)),
-        sem((2, DAP // 2)),
-        sem((2, 2)),
-        sem((2, DAP // 2)),
-        sem((2, DAP // 2)),
-        sem((2, DAP)),
-        sem((2, DAP)),
-        sem((2, DAP)),
-        sem((2, DAP)),
-        sem((2, DAP)),
+        sem((2,)),
+        sem((2,)),
+        sem((3, 2)),
+        sem((4,)),
+        sem((4,)),
+        sem((3,)),
+        sem((3,)),
+        sem((2,)),
+        sem((2,)),
     ]
+    whole = pl.BlockSpec(memory_space=pl.ANY)
+    held = pl.BlockSpec(memory_space=pltpu.VMEM)
     d_pair, small, grad_project, grad_out = pl.pallas_call(
         kernel,
         out_shape=(
@@ -816,15 +1011,26 @@
             jax.ShapeDtypeStruct((2, CHANNELS, 4 * CHANNELS), F32),
             jax.ShapeDtypeStruct((2, CHANNELS, CHANNELS), F32),
         ),
-        in_specs=[pl.BlockSpec(memory_space=pltpu.VMEM)] * 6,
-        out_specs=[pl.BlockSpec(memory_space=pltpu.VMEM)] * 4,
+        in_specs=[whole] * 6,
+        out_specs=[whole, held, whole, whole],
         scratch_shapes=scratch,
         compiler_params=pltpu.CompilerParams(
             collective_id=0, has_side_effects=True, vmem_limit_bytes=56 << 20
         ),
-    )(pair_rep, cotangent, norm_gain, w_project, w_bias_rows, w_out)
-    grad_bias = jnp.swapaxes(small[:, :HEADS], 1, 2)
-    return (d_pair, small[:, HEADS], grad_project, grad_bias, grad_out)
+    )(pair_rep, cotangent, norm_gain, w_project, jnp.swapaxes(w_bias, 1, 2), w_out)
+    outputs = pl.pallas_call(
+        finish_kernel,
+        out_shape=(
+            jax.ShapeDtypeStruct(cells, BF16),
+            jax.ShapeDtypeStruct((2, CHANNELS), F32),
+            jax.ShapeDtypeStruct((2, CHANNELS, 4 * CHANNELS), F32),
+            jax.ShapeDtypeStruct((2, HEADS, CHANNELS), F32),
+            jax.ShapeDtypeStruct((2, CHANNELS, CHANNELS), F32),
+        ),
+        in_specs=[pl.BlockSpec(memory_space=pltpu.VMEM)] * 4,
+        out_specs=[pl.BlockSpec(memory_space=pltpu.VMEM)] * 5,
+    )(d_pair, small, grad_project, grad_out)
+    return outputs[:3] + (jnp.swapaxes(outputs[3], 1, 2), outputs[4])
 
 
 def solution(mesh):

time: 136 us -> 113 us (0.83)
  Pallas kernels: 127 us -> 112 us
  local copies, waits for them, and re-layouts: 7.45 us -> 0 us
    pallas_call x1, Pallas kernels: 127 us -> 109 us  [per_device(): pl.pallas_call(kernel, out_shape=(jax.ShapeDtypeStruct(cells, BF16), jax....]
    unnamed x7 -> x0, local copies, waits for them, and re-layouts: 3.61 us -> none
    pallas_call x0 -> x1, Pallas kernels: none -> 2.28 us  [per_device(): pl.pallas_call(finish_kernel, out_shape=(jax.ShapeDtypeStruct(cells, BF16...]
where the time goes in v4:
time: 113 us; the launch traced here: 112 us
  Pallas kernels  112 us (99%)
    pallas_call x1, Pallas kernels, per_device(): pl.pallas_call(kernel, out_shape=(jax.ShapeDtypeStruct(cells, BF16), jax....  109 us
    pallas_call x1, Pallas kernels, per_device(): pl.pallas_call(finish_kernel, out_shape=(jax.ShapeDtypeStruct(cells, BF16...  2.28 us

profile of v4, /device:TPU:1, one launch (start us, length us, event | category | flops | bytes accessed | tf_op | source)
XLA Modules:
  0.0 112.4 jit_solution(7617952764268752173)
XLA Ops:
  0.6 109.5 %shard_map.101 = (bf16[8,256,128]{2,1,0:T(8,128)(2,1)}, f32[2,8,128]{2,1,0:T(8,128)}, f32[2,128,512]{2,1,0:T(8,128)}, f32[2,128,128]{2,1,0:T(8,128)}) custom-call(bf16[8,256,128]{2,1,0:T(8,128)(2,1)} %x_hbm.1, bf16[8,256,128]{2,1,0:T(8,128)(2,1)} %cot_hbm.1, f32[2,128]{1,0:T(2,128)} %gain_hbm.1, f32[2,128,512]{2,1,0:T(8,128)} %wp_hbm.1, ...), custom_call_target="tpu_custom_call" | custom-call | tf_op jit(solution)/shard_map/pallas_call | solution.py:1006
  110.1 2.3 %shard_map.102 = (bf16[8,256,128]{2,1,0:T(8,128)(2,1)}, f32[2,128]{1,0:T(2,128)}, f32[2,128,512]{2,1,0:T(8,128)}, f32[2,4,128]{2,1,0:T(4,128)}, f32[2,128,128]{2,1,0:T(8,128)}) custom-call(bf16[8,256,128]{2,1,0:T(8,128)(2,1)} %get-tuple-element.14.pair_ref, f32[2,8,128]{2,1,0:T(8,128)} %get-tuple-element.15.small_ref, ...), custom_call_target="tpu_custom_call" | custom-call | tf_op jit(solution)/shard_map/pallas_call | solution.py:1021

commit v5 on v4

--- a/solution.py
+++ b/solution.py
@@ -100,6 +100,7 @@
     o_s,
     mix_s,
     p_s,
+    scores_s,
     dproj_s,
     dkt_s,
     dvt_s,
@@ -180,7 +181,7 @@
             device_id_type=MESH,
         )
 
-    loop(1, DAP, tell)
+    loop(1, DAP, tell, 31)
 
     def load(src, dst, index):
         return pltpu.make_async_copy(src, dst, in_s.at[index])
@@ -254,15 +255,15 @@
         return remote(held, held, pass_ss.at[layer], pass_rs.at[layer], sibling)
 
     def near_start(layer):
-        loop(1, 8, lambda step: near_copy(layer, near(step)).start())
+        loop(1, 8, lambda step: near_copy(layer, near(step)).start(), 7)
 
     def far_start(layer):
         near_all(layer).wait_recv()
-        loop(1, 4, lambda step: far_copy(layer, turn(first_block, step)).start())
+        loop(1, 4, lambda step: far_copy(layer, turn(first_block, step)).start(), 3)
 
     def far_forward(layer):
         far_all(layer, far_ss, far_rs).wait_recv()
-        loop(1, 4, lambda step: far_pass(layer, turn(first_block, step)).start())
+        loop(1, 4, lambda step: far_pass(layer, turn(first_block, step)).start(), 3)
 
     def far_take(layer):
         far_all(layer, pass_ss, pass_rs).wait_recv()
@@ -333,9 +334,19 @@
                 at = head * BLOCK + part * ROWS
                 bias_q[at : at + ROWS, :] = piece[head * ROWS : (head + 1) * ROWS]
 
+    def products(layer):
+        def one_block(block):
+            def row(index):
+                queries = stack(q_s[layer, index, block_rows(block), :])
+                scores_s[index, block] = dot_nt(queries, k_s[layer, index])
+
+            loop(0, ROWS, row, ROWS)
+
+        loop(0, BLOCKS, one_block)
+
     def weights(layer, index, block):
         queries = stack(q_s[layer, index, block_rows(block), :])
-        scores = dot_nt(queries, k_s[layer, index]) + bias_q[...]
+        scores = scores_s[index, block] + bias_q[...]
         shifted = jnp.exp(scores - jnp.max(scores, axis=-1, keepdims=True))
         return queries, shifted * (1.0 / jnp.sum(shifted, axis=-1, keepdims=True))
 
@@ -502,7 +513,7 @@
 
     def wg_start():
         wg_add(0)
-        loop(1, DAP // 2, lambda step: wg_copy(other(2 * step)).start())
+        loop(1, DAP // 2, lambda step: wg_copy(other(2 * step)).start(), 5)
         wg_recv[mine] = wg_tot[0, tile(me), :]
 
     my_z = lax.rem(mine, 4)
@@ -648,7 +659,7 @@
         return remote(held, held, sg_ss.at[layer], sg_rs.at[layer], sibling)
 
     def small_start(layer):
-        loop(1, DAP, lambda step: small_copy(layer, other(step)).start())
+        loop(1, DAP, lambda step: small_copy(layer, other(step)).start(), 31)
 
     def weight_sums():
         tiles_all(wg_recv, 0).wait_recv()
@@ -656,7 +667,7 @@
         for chip in range(1, DAP // 2):
             total = total + wg_recv[chip]
         wg_all[core, mine] = total
-        loop(1, DAP // 2, lambda step: wa_copy(other(2 * step)).start())
+        loop(1, DAP // 2, lambda step: wa_copy(other(2 * step)).start(), 5)
 
     def small_out(layer):
         small_all(layer).wait_recv()
@@ -729,6 +740,7 @@
     cot_recv[me] = cot_send[me]
     pl.semaphore_wait(barrier, DAP - 1)
     near_start(0)
+    products(0)
 
     def cot_start(step):
         block = lax.rem(first_block + BLOCKS - step, BLOCKS)
@@ -736,6 +748,7 @@
             0,
             8,
             lambda part: swap_start(cot_send, cot_recv, cot_ss, cot_rs, block * 8 + part),
+            8,
         )
 
     far_start(0)
@@ -809,6 +822,7 @@
     far_forward(1)
     loop(2, BLOCKS, cot_start)
     project(1)
+    products(1)
     far_take(1)
     for head in range(HEADS):
         pieces = bias_all[1].astype(F32)[:, head * ROWS : (head + 1) * ROWS, :]
@@ -939,6 +953,7 @@
         vmem((2,) + cells, F32),
         vmem((2,) + cells, BF16),
         vmem((ROWS, BLOCKS, STACK, LENGTH), BF16),
+        vmem((ROWS, BLOCKS, STACK, LENGTH), F32),
         vmem((ROWS, LENGTH, 4 * CHANNELS), BF16),
         vmem((ROWS, CHANNELS, LENGTH), F32),
         vmem((ROWS, CHANNELS, LENGTH), F32),

time: 113 us -> 109 us (0.965)
  Pallas kernels: 112 us -> 108 us
    pallas_call x1, Pallas kernels: 109 us -> 106 us  [per_device(): pl.pallas_call(kernel, out_shape=(jax.ShapeDtypeStruct(cells, BF16), jax....]
where the time goes in v5:
time: 109 us
  Pallas kernels  108 us (99%)
    pallas_call x1, Pallas kernels, per_device(): pl.pallas_call(kernel, out_shape=(jax.ShapeDtypeStruct(cells, BF16), jax....  106 us
    pallas_call x1, Pallas kernels, per_device(): pl.pallas_call(finish_kernel, out_shape=(jax.ShapeDtypeStruct(cells, BF16...  2.28 us

profile of v5, /device:TPU:1, one launch (start us, length us, event | category | flops | bytes accessed | tf_op | source)
XLA Modules:
  0.0 109.0 jit_solution(7841245385309130399)
XLA Ops:
  0.6 106.1 %shard_map.101 = (bf16[8,256,128]{2,1,0:T(8,128)(2,1)}, f32[2,8,128]{2,1,0:T(8,128)}, f32[2,128,512]{2,1,0:T(8,128)}, f32[2,128,128]{2,1,0:T(8,128)}) custom-call(bf16[8,256,128]{2,1,0:T(8,128)(2,1)} %x_hbm.1, bf16[8,256,128]{2,1,0:T(8,128)(2,1)} %cot_hbm.1, f32[2,128]{1,0:T(2,128)} %gain_hbm.1, f32[2,128,512]{2,1,0:T(8,128)} %wp_hbm.1, ...), custom_call_target="tpu_custom_call" | custom-call | tf_op jit(solution)/shard_map/pallas_call | solution.py:1021
  106.8 2.3 %shard_map.102 = (bf16[8,256,128]{2,1,0:T(8,128)(2,1)}, f32[2,128]{1,0:T(2,128)}, f32[2,128,512]{2,1,0:T(8,128)}, f32[2,4,128]{2,1,0:T(4,128)}, f32[2,128,128]{2,1,0:T(8,128)}) custom-call(bf16[8,256,128]{2,1,0:T(8,128)(2,1)} %get-tuple-element.14.pair_ref, f32[2,8,128]{2,1,0:T(8,128)} %get-tuple-element.15.small_ref, ...), custom_call_target="tpu_custom_call" | custom-call | tf_op jit(solution)/shard_map/pallas_call | solution.py:1036
